TPU v7x, 32 devices: a whole 2x2x4 slice. The times are simulated.
32 devices in a mesh: ctx: 2 (over x), clu: 4 (over z), tp: 4 (over y, core).
Axes of the slice: x: 2, y: 2, z: 4, core: 2. Of those that a mesh axis runs over, the one named last changes fastest.
Arguments:
- tokens: bfloat16 [2, 1024, 4096], P('ctx', 'clu'), may hold values from -32 to 32
- proj_weight: bfloat16 [4096, 2, 2048], P(('ctx', 'clu'), None, 'tp'), may hold values from -0.09375 to 0.09375
- clusters: int32 [2, 1024, 16], P('ctx', 'clu', 'tp'), may hold values from 0 to 63, as said below
Outputs:
- attended: bfloat16 [2, 1024, 2048], P('ctx', 'clu', 'tp')
Inputs may be any that keep to these rules, and one draw needn't show every extreme that they name: `clusters`: owner k of head h holds ids k * 16 to (k + 1) * 16 - 1. In each aligned block of 256 positions of a sequence, for every head, at most 128 positions have ids of one owner; for each sequence and head one owner has exactly 128 positions in every block.
All inputs are finite; a program needn't handle non-finite values.
Results may differ from a plain program's by a relative error of at most 0.0068.
Values may be sent and summed in bfloat16 or wider, within the bound.
A program may use at most 64 MiB of HBM per device.

v0:
```python
import jax
import jax.numpy as jnp
from jax import lax
from jax.sharding import PartitionSpec as P

CLUSTERS = 64


def body(tokens, proj_weight, clusters):
    local_rows = tokens[0]
    row_count = local_rows.shape[0]
    owners = lax.axis_size("clu")
    heads_here = clusters.shape[2]
    proj_width = proj_weight.shape[2]
    head_dim = proj_width // heads_here
    capacity = 2 * row_count // owners
    per_owner = CLUSTERS // owners
    length = row_count * owners
    total_slots = owners * capacity
    score_scale = head_dim ** (-0.5)
    weight_piece = lax.all_gather(proj_weight, ("ctx", "clu"), axis=0, tiled=True)
    flat_piece = weight_piece.reshape(weight_piece.shape[0], 2 * proj_width)
    summed = jnp.dot(local_rows, flat_piece, preferred_element_type=jnp.float32)
    projected = summed.astype(jnp.bfloat16)
    queries = projected[:, :proj_width].reshape(row_count, heads_here, head_dim)
    values = projected[:, proj_width:].reshape(row_count, heads_here, head_dim)
    features = jnp.concatenate([queries, values], axis=2).transpose(1, 0, 2)
    cluster_ids = clusters[0]
    owner_of = cluster_ids // per_owner
    onehot = (owner_of[:, :, None] == jnp.arange(owners, dtype=jnp.int32)[None, None, :]).astype(
        jnp.int32
    )
    rank_in = jnp.sum((jnp.cumsum(onehot, axis=0) - onehot) * onehot, axis=2)
    slot_of = (owner_of * capacity + rank_in).T
    head_rows = jnp.arange(heads_here, dtype=jnp.int32)[:, None]
    token_index = jnp.broadcast_to(
        jnp.arange(row_count, dtype=jnp.int32)[None, :], (heads_here, row_count)
    )
    source = jnp.zeros((heads_here, total_slots), jnp.int32).at[head_rows, slot_of].set(token_index)
    positions = lax.axis_index("clu") * row_count + jnp.arange(row_count, dtype=jnp.int32)
    labels = cluster_ids.T * length + positions[None, :]
    slot_tags = (
        jnp.full((heads_here, total_slots), -1, jnp.int32).at[head_rows, slot_of].set(labels)
    )
    outgoing = jnp.take_along_axis(features, source[:, :, None], axis=1)
    outgoing = jnp.where((slot_tags >= 0)[:, :, None], outgoing, jnp.zeros_like(outgoing))
    outgoing = outgoing.reshape(heads_here, owners, capacity, 2 * head_dim)
    slot_tags = slot_tags.reshape(heads_here, owners, capacity)

    def attend_head(head_item):
        slot_block, key_tags = head_item
        flattened = slot_block.reshape(-1, 2 * head_dim)
        key_rows = flattened[:, :head_dim]
        value_rows = flattened[:, head_dim:]
        key_tags = key_tags.reshape(-1)
        scores = (
            jnp.einsum("qd,kd->qk", key_rows, key_rows, preferred_element_type=jnp.float32)
            * score_scale
        )
        tag_group = key_tags // length
        tag_pos = key_tags % length
        admitted = (
            (key_tags[None, :] >= 0)
            & (tag_group[None, :] == tag_group[:, None])
            & (tag_pos[None, :] <= tag_pos[:, None])
        )
        scores = jnp.where(key_tags[None, :] == key_tags[:, None], -100000.0, scores)
        scores = jnp.where(admitted, scores, -1e30)
        row_max = jnp.max(scores, axis=1, keepdims=True)
        exp_scores = jnp.exp(scores - row_max)
        row_total = jnp.sum(exp_scores, axis=1, keepdims=True)
        probabilities = (exp_scores / row_total).astype(jnp.bfloat16)
        result = jnp.dot(probabilities, value_rows, preferred_element_type=jnp.float32).astype(
            jnp.bfloat16
        )
        return result.reshape(slot_block.shape[0], slot_block.shape[1], head_dim)

    replies = lax.map(
        attend_head,
        (
            lax.all_to_all(outgoing, "clu", split_axis=1, concat_axis=1, tiled=True),
            lax.all_to_all(slot_tags, "clu", split_axis=1, concat_axis=1, tiled=True),
        ),
    )
    returned = lax.all_to_all(replies, "clu", split_axis=1, concat_axis=1, tiled=True)
    returned = returned.reshape(heads_here, total_slots, head_dim)
    gathered = jnp.take_along_axis(returned, slot_of[:, :, None], axis=1)
    return gathered.transpose(1, 0, 2).reshape(1, row_count, heads_here * head_dim)


def solution(mesh):
    return jax.shard_map(
        body,
        mesh=mesh,
        in_specs=(P("ctx", "clu", None), P(("ctx", "clu"), None, "tp"), P("ctx", "clu", "tp")),
        out_specs=P("ctx", "clu", "tp"),
        check_vma=False,
    )
```

profile of v0, /device:TPU:0, one launch (start us, length us, event | category | flops | bytes accessed | tf_op | source)
XLA Modules:
  0.0 243.7 jit_solution(14250623694650654107)
XLA Ops:
  6.5 0.0 copy-start
  6.5 0.0 all-gather.2.cloned.1.call-start
  6.5 0.7 all-gather.2.cloned.1.call-update
  7.3 0.7 fusion.21
  8.0 4.8 %reduce-window.6 = s32[4,4,2,128]{3,2,1,0:T(2,128)S(1)} reduce-window(s32[4,4,2,128]{3,2,1,0:T(2,128)S(1)} %compare_convert_fusion, s32[]{:T(128)} %copy.56), window={size=1x1x1x128 pad=0_0x0_0x0_0x127_0}, to_apply=%region_0.1 | reduce-window | flops 520192 | bytes 32772 | tf_op jit(solution)/shard_map/reduce-window
  12.8 0.1 slice.34
  12.9 0.1 copy.19
  13.1 0.1 copy.20
  13.2 0.1 broadcast_add_fusion
  13.4 0.7 multiply_reduce_fusion
  14.1 0.7 and_reduce_fusion
  14.9 4.3 %scatter_custom_fusion = s32[2048]{0:T(1024)S(1)} fusion(s32[1024]{0:T(1024)S(1)} %bitcast.120, s32[1024]{0:T(1024)S(1)} %bitcast.119, s32[]{:T(128)} %constant.139.clone.1), kind=kCustom, calls=%fused_computation.69 | custom fusion | bytes 8196
  19.2 0.6 copy.21
  19.8 6.3 %all-to-all-start = ((s32[4,4,128]{2,0,1:T(4,128)}), s32[4,4,128]{2,0,1:T(4,128)S(1)}, u32[]{:S(2)}, u32[]{:S(2)}) async-start(s32[4,4,128]{2,0,1:T(4,128)} %copy.21), calls=%async_computation | async-start | bytes 16384 | tf_op jit(solution)/shard_map/all_to_all | solution.py:82
  26.1 4.3 %scatter_custom_fusion.1 = s32[2048]{0:T(1024)S(1)} fusion(s32[1024]{0:T(1024)S(1)} %bitcast.121, s32[1024]{0:T(1024)S(1)} %bitcast.122, s32[]{:T(128)} %copy.56), kind=kCustom, calls=%fused_computation.66 | custom fusion | bytes 8196
  30.5 106.8 %all-gather.2.cloned.1.call-done = bf16[4096,2,512]{2,1,0:T(2,128)(2,1)} async-done(((bf16[512,2,512]{2,1,0:T(2,128)(2,1)}), bf16[4096,2,512]{2,1,0:T(2,128)(2,1)}) %all-gather.2.cloned.1.call-update) | async-done | bytes 8388624 | tf_op jit(solution)/shard_map/all_gather | solution.py:21
  137.3 9.3 %copy.40 = bf16[512,8,2,512]{3,1,2,0:T(8,128)(2,1)} copy(bf16[512,8,2,512]{3,2,1,0:T(2,128)(2,1)} %bitcast.106) | data formatting | bytes 16777216
  146.6 5.7 %fusion.8 = bf16[256,1024]{1,0:T(8,128)(2,1)S(1)} fusion(bf16[4096,1024]{1,0:T(8,128)(2,1)} %bitcast.107, bf16[1,256,4096]{2,1,0:T(8,128)(2,1)S(1)} %copy-done), kind=kOutput, calls=%fused_computation.27 | convolution fusion | flops 2147745792 | bytes 11010048 | tf_op jit(solution)/shard_map/dot_general | solution.py:23
  152.4 0.1 copy_bitcast_fusion
  152.5 0.1 maximum_bitcast_fusion
  152.6 20.6 %gather_fusion = bf16[2048,256]{1,0:T(8,128)(2,1)} fusion(bf16[4,256,256]{2,1,0:T(8,128)(2,1)S(1)} %maximum_bitcast_fusion, s32[2048]{0:T(1024)S(1)} %bitcast.103), kind=kCustom, calls=%fused_computation | custom fusion | bytes 2113536 | tf_op jit(solution)/shard_map/jit(take_along_axis)/gather | solution.py:45
  173.2 2.6 %fusion.11 = bf16[4,4,128,256]{3,2,0,1:T(8,128)(2,1)} fusion(bf16[4,4,128,256]{3,2,1,0:T(8,128)(2,1)} %bitcast.110, pred[4,4,128]{2,0,1:T(4,128)(4,1)S(1)} %and_bitcast_fusion, pred[4,4,128]{2,0,1:T(4,128)(4,1)S(1)} %copy.22), kind=kLoop, calls=%fused_computation.29 | loop fusion | flops 1048576 | bytes 2101248 | tf_op jit(solution)/shard_map/jit(_where)/select_n | solution.py:46
  175.7 0.0 all-to-all-done
  175.7 3.5 %all-to-all-start.1 = ((bf16[4,4,128,256]{3,2,0,1:T(8,128)(2,1)}), bf16[4,4,128,256]{3,2,0,1:T(8,128)(2,1)S(1)}, u32[]{:S(2)}, u32[]{:S(2)}) async-start(bf16[4,4,128,256]{3,2,0,1:T(8,128)(2,1)} %fusion.11), calls=%async_computation.1 | async-start | bytes 2097152 | tf_op jit(solution)/shard_map/all_to_all | solution.py:81
  179.3 25.6 %all-to-all-done.1 = bf16[4,4,128,256]{3,2,0,1:T(8,128)(2,1)S(1)} async-done(((bf16[4,4,128,256]{3,2,0,1:T(8,128)(2,1)}), bf16[4,4,128,256]{3,2,0,1:T(8,128)(2,1)S(1)}, u32[]{:S(2)}, u32[]{:S(2)}) %all-to-all-start.1) | async-done | bytes 1048608 | tf_op jit(solution)/shard_map/all_to_all | solution.py:81
  204.8 7.5 %while.12 = (s32[]{:T(128)}, bf16[4,4,128,128]{3,2,0,1:T(8,128)(2,1)}, s32[4,4,128]{2,0,1:T(4,128)S(1)}, bf16[4,4,128,256]{3,2,0,1:T(8,128)(2,1)S(1)}, s32[]{:T(128)}) while((s32[]{:T(128)}, bf16[4,4,128,128]{3,2,0,1:T(8,128)(2,1)}, s32[4,4,128]{2,0,1:T(4,128)S(1)}, bf16[4,4,128,256]{3,2,0,1:T(8,128)(2,1)S(1)}, s32[]{:T(128)}) %tuple.38), condition=%wide.region_8.9_spmd, body=%wide.region_5.8_spmd.sunk | while | flops 137962496 | bytes 4361297 | solution.py:78
  204.9 0.6 fusion.34
  205.4 0.2 fusion.35
  205.6 0.4 convolution_convert_fusion.2
  206.0 0.7 constant_dynamic-update-slice_fusion.2
  206.8 0.5 fusion.34
  207.3 0.2 fusion.35
  207.5 0.4 convolution_convert_fusion.2
  207.9 0.7 constant_dynamic-update-slice_fusion.2
  208.6 0.5 fusion.34
  209.2 0.2 fusion.35
  209.4 0.4 convolution_convert_fusion.2
  209.8 0.7 constant_dynamic-update-slice_fusion.2
  210.5 0.5 fusion.34
  211.0 0.2 fusion.35
  211.2 0.4 convolution_convert_fusion.2
  211.6 0.7 constant_dynamic-update-slice_fusion.2
  212.3 3.5 %all-to-all-start.2 = ((bf16[4,4,128,128]{3,2,0,1:T(8,128)(2,1)}), bf16[4,4,128,128]{3,2,0,1:T(8,128)(2,1)S(1)}, u32[]{:S(2)}, u32[]{:S(2)}) async-start(bf16[4,4,128,128]{3,2,0,1:T(8,128)(2,1)} %get-tuple-element.61), calls=%async_computation.2 | async-start | bytes 1048576 | tf_op jit(solution)/shard_map/all_to_all | solution.py:85
  215.8 13.9 %all-to-all-done.2 = bf16[4,4,128,128]{3,2,0,1:T(8,128)(2,1)S(1)} async-done(((bf16[4,4,128,128]{3,2,0,1:T(8,128)(2,1)}), bf16[4,4,128,128]{3,2,0,1:T(8,128)(2,1)S(1)}, u32[]{:S(2)}, u32[]{:S(2)}) %all-to-all-start.2) | async-done | bytes 524320 | tf_op jit(solution)/shard_map/all_to_all | solution.py:85
  229.8 5.8 %gather_fusion.1 = bf16[1024,128]{1,0:T(8,128)(2,1)S(1)} fusion(bf16[4,512,128]{2,1,0:T(8,128)(2,1)S(1)} %bitcast.105, s32[1024]{0:T(1024)S(1)} %bitcast.104), kind=kCustom, calls=%fused_computation.1 | custom fusion | bytes 532480 | tf_op jit(solution)/shard_map/jit(take_along_axis)/gather | solution.py:87
  235.6 0.2 broadcast_select_fusion
  235.8 0.2 copy.30
  236.0 0.8 reshape.223
  (42 shorter events, 0.5 us)
Async XLA Ops:
  6.5 140.1 %copy-start = (bf16[1,256,4096]{2,1,0:T(8,128)(2,1)S(1)}, bf16[1,256,4096]{2,1,0:T(8,128)(2,1)}, u32[]{:S(2)}) copy-start(bf16[1,256,4096]{2,1,0:T(8,128)(2,1)} %param.5) | copy-start | bytes 6291460
  6.5 130.8 %all-gather.2.cloned.1.call-start = ((), (), s32[]{:S(2)}) async-start(), calls=%async_computation.3 | async-start | bytes 9437184 | tf_op jit(solution)/shard_map/all_gather | solution.py:21
  19.8 155.9 %all-to-all-start = ((s32[4,4,128]{2,0,1:T(4,128)}), s32[4,4,128]{2,0,1:T(4,128)S(1)}, u32[]{:S(2)}, u32[]{:S(2)}) async-start(s32[4,4,128]{2,0,1:T(4,128)} %copy.21), calls=%async_computation | async-start | bytes 16384 | tf_op jit(solution)/shard_map/all_to_all | solution.py:82
  175.7 29.1 %all-to-all-start.1 = ((bf16[4,4,128,256]{3,2,0,1:T(8,128)(2,1)}), bf16[4,4,128,256]{3,2,0,1:T(8,128)(2,1)S(1)}, u32[]{:S(2)}, u32[]{:S(2)}) async-start(bf16[4,4,128,256]{3,2,0,1:T(8,128)(2,1)} %fusion.11), calls=%async_computation.1 | async-start | bytes 2097152 | tf_op jit(solution)/shard_map/all_to_all | solution.py:81
  212.3 17.4 %all-to-all-start.2 = ((bf16[4,4,128,128]{3,2,0,1:T(8,128)(2,1)}), bf16[4,4,128,128]{3,2,0,1:T(8,128)(2,1)S(1)}, u32[]{:S(2)}, u32[]{:S(2)}) async-start(bf16[4,4,128,128]{3,2,0,1:T(8,128)(2,1)} %get-tuple-element.61), calls=%async_computation.2 | async-start | bytes 1048576 | tf_op jit(solution)/shard_map/all_to_all | solution.py:85
Sparse Core Ops, SparseCore 0:
  9.5 127.7 all-gather.1
where the time goes:
time: 244 us
  waiting for transfers between devices  147 us (60%)
  local copies, waits for them, and re-layouts  49.4 us (20%)
  between operations  13.6 us (6%)
  starting transfers between devices  13.3 us (5%)
  other arithmetic  10.9 us (4%)
  matrix products  9.38 us (4%)
    all_gather x1, waiting for transfers between devices, body(): lax.all_gather(proj_weight, ('ctx', 'clu'), axis=0, tiled=True)  107 us
    all_to_all x1, waiting for transfers between devices, body(): lax.all_to_all(outgoing, 'clu', split_axis=1, concat_axis=1, tiled=True)  25.6 us
    gather x1, local copies, waits for them, and re-layouts, body(): outgoing = jnp.take_along_axis(features, source[:, :, None], axis=1)  20.6 us
    unnamed x12, local copies, waits for them, and re-layouts  18 us
    all_to_all x1, waiting for transfers between devices, body(): lax.all_to_all(replies, 'clu', split_axis=1, concat_axis=1, tiled=True)  13.9 us
    all_to_all x1, starting transfers between devices, body(): lax.all_to_all(slot_tags, 'clu', split_axis=1, concat_axis=1, tiled=True)  6.32 us
    gather x1, local copies, waits for them, and re-layouts, body(): gathered = jnp.take_along_axis(returned, slot_of[:, :, None], axis=1)  5.83 us
    dot_general x1, matrix products, body(): summed = jnp.dot(local_rows, flat_piece, preferred_element_type=jnp.float32)  5.71 us
  transfers between devices with their start and end apart: 4, of which 3 were waited for; matrix products, arithmetic and copies ran while one was open for 23% of the time, Pallas kernels for 0%

commit v1 on v0

--- a/solution.py
+++ b/solution.py
@@ -1,9 +1,286 @@
+import functools
+
 import jax
 import jax.numpy as jnp
 from jax import lax
+from jax.experimental import pallas as pl
+from jax.experimental.pallas import tpu as pltpu
 from jax.sharding import PartitionSpec as P
 
 CLUSTERS = 64
+MESH = pl.DeviceIdType.MESH
+
+
+def head_kernel(
+    owners, depth, head_dim, score_scale,
+    tok_ref, w_ref, cl_ref, out_ref,
+    rows, weights, ids, proj, reply,
+    own_sem, wz_send, wz_recv, wx_send, wx_recv, id_send, id_recv,
+    hop_send, hop_recv, core_send, core_recv, y_send, y_recv, far_send, far_recv,
+    out_send, out_recv,
+):
+    a = lax.axis_index("ctx")
+    c = lax.axis_index("clu")
+    t = lax.axis_index("tp")
+    k = lax.rem(t, 2)
+    y = t // 2
+    count = tok_ref.shape[0]
+    quarter = tok_ref.shape[1] // 4
+    last = owners - 1
+    core_peer = {"tp": y * 2 + 1 - k}
+    y_peer = {"tp": (1 - y) * 2 + k}
+    x_peer = {"ctx": 1 - a}
+
+    def at_clu(index):
+        return {"clu": index}
+
+    def remote(src, dst, send, recv, peer):
+        return pltpu.make_async_remote_copy(
+            src_ref=src, dst_ref=dst, send_sem=send, recv_sem=recv,
+            device_id=peer, device_id_type=MESH,
+        )
+
+    def features(q):
+        return pl.ds(pl.multiple_of(q * quarter, quarter), quarter)
+
+    def piece(ctx, clu):
+        return weights.at[pl.ds(pl.multiple_of((ctx * owners + clu) * depth, depth), depth)]
+
+    barrier = pltpu.get_barrier_semaphore()
+    others = [at_clu(lax.rem(c + d, owners)) for d in range(1, owners)]
+    others += [core_peer, y_peer, x_peer]
+    for peer in others:
+        pl.semaphore_signal(barrier, inc=1, device_id=peer, device_id_type=MESH)
+    own_rows = pltpu.make_async_copy(tok_ref, rows.at[c], own_sem.at[0])
+    own_piece = pltpu.make_async_copy(w_ref.at[c], piece(a, c), own_sem.at[1])
+    own_ids = pltpu.make_async_copy(cl_ref.at[c], ids.at[c], own_sem.at[2])
+    for copy in (own_rows, own_piece, own_ids):
+        copy.start()
+    pl.semaphore_wait(barrier, len(others))
+
+    def hop(side, step):
+        block = c - step if side == 0 else c + step
+        src = rows.at[block, :, features(t)] if step else tok_ref.at[:, features(t)]
+        return remote(
+            src, rows.at[block, :, features(t)],
+            hop_send.at[side, step], hop_recv.at[side, step],
+            at_clu(c + 1 if side == 0 else c - 1),
+        )
+
+    def hop_sends(side, step):
+        if side == 0:
+            return (c >= step) & (c < last)
+        return (c + step <= last) & (c > 0)
+
+    def came(side, step):
+        block = c - 1 - step if side == 0 else c + 1 + step
+        return block, ((block >= 0) if side == 0 else (block <= last))
+
+    def landed(block, q, send, recv, peer):
+        here = rows.at[block, :, features(q)]
+        return remote(here, here, send, recv, peer)
+
+    def to_core(side, step, block, q):
+        return landed(block, q, core_send.at[side, step], core_recv.at[side, step], core_peer)
+
+    def to_y(side, step, block, q):
+        return landed(block, q, y_send.at[side, step], y_recv.at[side, step], y_peer)
+
+    def to_core_far(side, step, block, q):
+        return landed(block, q, far_send.at[side, step], far_recv.at[side, step], core_peer)
+
+    def w_hop(d):
+        goal = lax.rem(c + d, owners)
+        return remote(w_ref.at[goal], piece(a, c), wz_send.at[d - 1], wz_recv.at[d - 1], at_clu(goal))
+
+    def w_came(d):
+        source = lax.rem(c + owners - d, owners)
+        here = piece(a, source)
+        return remote(here, here, wz_send.at[d - 1], wz_recv.at[d - 1], at_clu(source))
+
+    def w_cross(d, ctx):
+        here = piece(ctx, lax.rem(c + owners - d, owners))
+        src = w_ref.at[c] if d == 0 else here
+        return remote(src, here, wx_send.at[d], wx_recv.at[d], x_peer)
+
+    def id_hop(d):
+        goal = lax.rem(c + d, owners)
+        return remote(cl_ref.at[goal], ids.at[c], id_send.at[d - 1], id_recv.at[d - 1], at_clu(goal))
+
+    def id_came(d):
+        source = lax.rem(c + owners - d, owners)
+        return remote(ids.at[source], ids.at[source], id_send.at[d - 1], id_recv.at[d - 1], at_clu(source))
+
+    for side in range(2):
+        pl.when(hop_sends(side, 0))(lambda side=side: hop(side, 0).start())
+    w_cross(0, a).start()
+    for d in range(1, owners):
+        w_hop(d).start()
+    for d in range(1, owners):
+        id_hop(d).start()
+
+    def project(block):
+        summed = jnp.dot(rows[block], weights[...], preferred_element_type=jnp.float32)
+        proj[block] = summed.astype(jnp.bfloat16)
+
+    def arrive(step):
+        for side in range(2):
+            block, here = came(side, step)
+
+            @pl.when(here)
+            def _(side=side, block=block):
+                landed(block, t, hop_send.at[side, step], hop_recv.at[side, step], core_peer).wait_recv()
+                to_y(side, step, block, t).start()
+                to_core(side, step, block, t).start()
+
+            if step + 1 < last:
+                pl.when(hop_sends(side, step + 1))(lambda side=side: hop(side, step + 1).start())
+        w_came(step + 1).wait_recv()
+        w_cross(step + 1, a).start()
+
+    def relay(step):
+        for side in range(2):
+            block, here = came(side, step)
+
+            @pl.when(here)
+            def _(side=side, block=block):
+                to_y(side, step, block, (1 - y) * 2 + k).wait_recv()
+                to_core_far(side, step, block, (1 - y) * 2 + k).start()
+
+    def finish(step):
+        for side in range(2):
+            block, here = came(side, step)
+
+            @pl.when(here)
+            def _(side=side, block=block):
+                to_core(side, step, block, y * 2 + 1 - k).wait_recv()
+                to_core_far(side, step, block, (1 - y) * 2 + 1 - k).wait_recv()
+                project(block)
+
+    for step in range(last):
+        arrive(step)
+        if step > 0:
+            relay(step - 1)
+    for copy in (own_rows, own_piece, own_ids):
+        copy.wait()
+    for d in range(owners):
+        w_cross(d, 1 - a).wait_recv()
+    project(c)
+    for step in range(last):
+        if step == last - 1:
+            relay(step)
+        finish(step)
+    for d in range(1, owners):
+        id_came(d).wait_recv()
+
+    def send_reply(goal):
+        return remote(
+            reply.at[goal], out_ref.at[:, pl.ds(pl.multiple_of(c * head_dim, head_dim), head_dim)],
+            out_send.at[goal], out_recv.at[c], at_clu(goal),
+        )
+
+    def keep_reply(goal):
+        return pltpu.make_async_copy(
+            reply.at[goal], out_ref.at[:, pl.ds(pl.multiple_of(c * head_dim, head_dim), head_dim)],
+            out_send.at[goal],
+        )
+
+    for goal in reversed(range(owners)):
+        query = proj[goal, :, :head_dim]
+        query_ids = jnp.transpose(ids[goal])[:, :1]
+        parts = []
+        for block in range(goal + 1):
+            scores = lax.dot_general(
+                query, proj[block, :, :head_dim], (((1,), (1,)), ((), ())),
+                preferred_element_type=jnp.float32,
+            ) * score_scale
+            admitted = query_ids == ids[block, :1, :]
+            if block == goal:
+                at = lax.broadcasted_iota(jnp.int32, (count, count), 0)
+                to = lax.broadcasted_iota(jnp.int32, (count, count), 1)
+                scores = jnp.where(at == to, -100000.0, scores)
+                admitted = admitted & (to <= at)
+            parts.append(jnp.where(admitted, scores, -1e30))
+        top = functools.reduce(jnp.maximum, [jnp.max(p, axis=1, keepdims=True) for p in parts])
+        total = jnp.zeros((count, 1), jnp.float32)
+        mixed = jnp.zeros((count, head_dim), jnp.float32)
+        for block, part in enumerate(parts):
+            part = jnp.exp(part - top)
+            total += jnp.sum(part, axis=1, keepdims=True)
+            mixed += jnp.dot(
+                part.astype(jnp.bfloat16), proj[block, :, head_dim:],
+                preferred_element_type=jnp.float32,
+            )
+        reply[goal] = (mixed / total).astype(jnp.bfloat16)
+        pl.when(c != goal)(lambda goal=goal: send_reply(goal).start())
+        pl.when(c == goal)(lambda goal=goal: keep_reply(goal).start())
+
+    for step in range(last):
+        for side in range(2):
+            block, here = came(side, step)
+            pl.when(hop_sends(side, step))(lambda side=side, step=step: hop(side, step).wait_send())
+
+            @pl.when(here)
+            def _(side=side, step=step, block=block):
+                to_y(side, step, block, t).wait_send()
+                to_core(side, step, block, t).wait_send()
+                to_core_far(side, step, block, (1 - y) * 2 + k).wait_send()
+
+    for d in range(1, owners):
+        w_hop(d).wait_send()
+        id_hop(d).wait_send()
+    for d in range(owners):
+        w_cross(d, a).wait_send()
+    for goal in range(owners):
+        @pl.when(c != goal)
+        def _(goal=goal):
+            send_reply(goal).wait_send()
+            column = out_ref.at[:, pl.ds(goal * head_dim, head_dim)]
+            remote(reply.at[goal], column, out_send.at[goal], out_recv.at[goal], at_clu(goal)).wait_recv()
+
+        pl.when(c == goal)(lambda goal=goal: keep_reply(goal).wait())
+
+
+def head_body(tokens, proj_weight, clusters):
+    row_count, width = tokens.shape[1:]
+    owners = lax.axis_size("clu")
+    heads_here = clusters.shape[2]
+    depth, _, proj_width = proj_weight.shape
+    head_dim = proj_width // heads_here
+    pieces = (
+        proj_weight.reshape(depth, 2, heads_here, head_dim)
+        .transpose(2, 0, 1, 3)
+        .reshape(heads_here, depth, 2 * head_dim)
+    )
+    labels = jnp.broadcast_to(clusters[0].T[:, None, :], (heads_here, 8, row_count))
+    steps = owners - 1
+    dma = pltpu.SemaphoreType.DMA
+    out = pl.pallas_call(
+        functools.partial(head_kernel, owners, depth, head_dim, head_dim ** (-0.5)),
+        out_shape=jax.ShapeDtypeStruct((row_count, proj_width), jnp.bfloat16),
+        in_specs=[pl.BlockSpec(memory_space=pl.ANY)] * 3,
+        out_specs=pl.BlockSpec(memory_space=pl.ANY),
+        scratch_shapes=[
+            pltpu.VMEM((owners, row_count, width), jnp.bfloat16),
+            pltpu.VMEM((width, 2 * head_dim), jnp.bfloat16),
+            pltpu.VMEM((owners, 8, row_count), jnp.int32),
+            pltpu.VMEM((owners, row_count, 2 * head_dim), jnp.bfloat16),
+            pltpu.VMEM((owners, row_count, head_dim), jnp.bfloat16),
+            dma((3,)),
+            dma((steps,)), dma((steps,)),
+            dma((owners,)), dma((owners,)),
+            dma((steps,)), dma((steps,)),
+            dma((2, steps)), dma((2, steps)),
+            dma((2, steps)), dma((2, steps)),
+            dma((2, steps)), dma((2, steps)),
+            dma((2, steps)), dma((2, steps)),
+            dma((owners,)), dma((owners,)),
+        ],
+        compiler_params=pltpu.CompilerParams(
+            collective_id=0, has_side_effects=True, vmem_limit_bytes=40 * 1024 * 1024
+        ),
+    )(tokens[0], pieces, labels)
+    return out[None]
 
 
 def body(tokens, proj_weight, clusters):
@@ -89,8 +366,11 @@
 
 
 def solution(mesh):
+    sizes = dict(mesh.shape)
+    heads_here = 16 // sizes["tp"]
+    by_head = sizes["ctx"] == 2 and sizes["tp"] == 4 and sizes["clu"] == heads_here
     return jax.shard_map(
-        body,
+        head_body if by_head else body,
         mesh=mesh,
         in_specs=(P("ctx", "clu", None), P(("ctx", "clu"), None, "tp"), P("ctx", "clu", "tp")),
         out_specs=P("ctx", "clu", "tp"),

time: 244 us -> 90.9 us (0.37)
  waiting for transfers between devices: 147 us -> 0 us
  Pallas kernels: 0 us -> 85.1 us
  local copies, waits for them, and re-layouts: 49.4 us -> 4.95 us
  between operations: 13.6 us -> 0.05 us
  starting transfers between devices: 13.3 us -> 0 us
  other arithmetic: 10.9 us -> 0 us
  matrix products: 9.38 us -> 0 us
    all_gather x1 -> x0, waiting for transfers between devices: 107 us -> none  [body(): lax.all_gather(proj_weight, ('ctx', 'clu'), axis=0, tiled=True)]
    pallas_call x0 -> x1, Pallas kernels: none -> 85.1 us  [head_body(): pl.pallas_call(functools.partial(head_kernel, owners, depth, head_dim, he...]
    all_to_all x3 -> x0, waiting for transfers between devices: 39.5 us -> none  [the longest x1 25.6 us: body(): lax.all_to_all(outgoing, 'clu', split_axis=1, concat_axis=1, tiled=True)]
    gather x2 -> x0, local copies, waits for them, and re-layouts: 26.4 us -> none  [the longest x1 20.6 us: body(): outgoing = jnp.take_along_axis(features, source[:, :, None], axis=1)]
    unnamed x12 -> x7, local copies, waits for them, and re-layouts: 18 us -> 3.52 us
    all_to_all x3 -> x0, starting transfers between devices: 13.3 us -> none  [the longest x1 6.32 us: body(): lax.all_to_all(slot_tags, 'clu', split_axis=1, concat_axis=1, tiled=True)]
    dot_general x9 -> x0, matrix products: 9.38 us -> none  [the longest x1 5.71 us: body(): summed = jnp.dot(local_rows, flat_piece, preferred_element_type=jnp.float32)]
    another operation x3 -> x0, other arithmetic: 4.93 us -> none
  transfers between devices with their start and end apart: 4 -> 0, of which waited for: 3 -> 0; matrix products, arithmetic and copies ran while one was open for 23% -> 0% of each run, Pallas kernels for 0% -> 0%
where the time goes in v1:
time: 90.9 us; the launch traced here: 90.1 us
  Pallas kernels  85.1 us (94%)
  local copies, waits for them, and re-layouts  4.95 us (5%)
    pallas_call x1, Pallas kernels, head_body(): pl.pallas_call(functools.partial(head_kernel, owners, depth, head_dim, he...  85.1 us
    unnamed x7, local copies, waits for them, and re-layouts  3.52 us

profile of v1, /device:TPU:0, one launch (start us, length us, event | category | flops | bytes accessed | tf_op | source)
XLA Modules:
  0.0 90.1 jit_solution(8354647179538635386)
XLA Ops:
  0.0 0.0 copy-start
  0.0 0.0 copy-start.2
  0.0 1.2 %copy-done = bf16[512,2,512]{2,1,0:T(2,128)(2,1)S(1)} copy-done((bf16[512,2,512]{2,1,0:T(2,128)(2,1)S(1)}, bf16[512,2,512]{2,1,0:T(2,128)(2,1)}, u32[]{:S(2)}) %copy-start) | copy-done | bytes 1048600
  1.2 0.7 bitcast_bitcast_fusion
  2.0 0.7 reshape.8.w_ref
  2.7 0.0 copy-done.2
  2.7 0.0 copy-start.1
  2.7 1.6 %copy-done.1 = bf16[1,256,4096]{2,1,0:T(8,128)(2,1)S(1)} copy-done((bf16[1,256,4096]{2,1,0:T(8,128)(2,1)S(1)}, bf16[1,256,4096]{2,1,0:T(8,128)(2,1)}, u32[]{:S(2)}) %copy-start.1) | copy-done | bytes 2097176
  4.3 85.1 %shard_map.37 = bf16[256,512]{1,0:T(8,128)(2,1)S(1)} custom-call(bf16[256,4096]{1,0:T(8,128)(2,1)S(1)} %bitcast.12, bf16[4,512,256]{2,1,0:T(8,128)(2,1)S(1)} %reshape.8.w_ref, s32[4,8,256]{2,1,0:T(8,128)S(1)} %broadcast_in_dim.4.cl_ref), custom_call_target="tpu_custom_call" | custom-call | tf_op jit(solution)/shard_map/pallas_call | solution.py:258
  89.4 0.7 copy.8
  (1 shorter events, 0.0 us)
Async XLA Ops:
  0.0 1.2 %copy-start = (bf16[512,2,512]{2,1,0:T(2,128)(2,1)S(1)}, bf16[512,2,512]{2,1,0:T(2,128)(2,1)}, u32[]{:S(2)}) copy-start(bf16[512,2,512]{2,1,0:T(2,128)(2,1)} %param.4) | copy-start | bytes 3145732
  0.0 2.7 %copy-start.2 = (s32[1,256,4]{1,2,0:T(4,128)S(1)}, s32[1,256,4]{1,2,0:T(4,128)}, u32[]{:S(2)}) copy-start(s32[1,256,4]{1,2,0:T(4,128)} %param.5) | copy-start | bytes 12292
  2.7 1.6 %copy-start.1 = (bf16[1,256,4096]{2,1,0:T(8,128)(2,1)S(1)}, bf16[1,256,4096]{2,1,0:T(8,128)(2,1)}, u32[]{:S(2)}) copy-start(bf16[1,256,4096]{2,1,0:T(8,128)(2,1)} %param.3) | copy-start | bytes 6291460

commit v2 on v1

v2 whole, which is shorter than its diff:
```python
import functools

import jax
import jax.numpy as jnp
from jax import lax
from jax.experimental import pallas as pl
from jax.experimental.pallas import tpu as pltpu
from jax.sharding import PartitionSpec as P

CLUSTERS = 64
MESH = pl.DeviceIdType.MESH


def head_kernel(
    owners, depth, head_dim, score_scale,
    tok_ref, w_ref, cl_ref, out_ref,
    rows, weights, ids, mine, part, theirs, proj, reply,
    own_sem, wm_send, wm_recv, wx_send, wx_recv, id_send, id_recv,
    cross_send, cross_recv, fwd_send, fwd_recv, mate_send, mate_recv,
    core_send, core_recv, y_send, y_recv, far_send, far_recv,
    part_send, part_recv, out_send, out_recv,
):
    a = lax.axis_index("ctx")
    c = lax.axis_index("clu")
    t = lax.axis_index("tp")
    k = lax.rem(t, 2)
    y = t // 2
    pair = c // 2
    side = lax.rem(c, 2)
    near = side != pair
    count = tok_ref.shape[0]
    half = tok_ref.shape[1] // 2
    run = half // 2
    quarter = half // 4
    core_peer = {"tp": y * 2 + 1 - k}
    y_peer = {"tp": (1 - y) * 2 + k}
    x_peer = {"ctx": 1 - a}
    mate = pair * 2 + 1 - side
    twin = (1 - pair) * 2 + side

    def at_clu(index):
        return {"clu": index}

    def remote(src, dst, send, recv, peer):
        return pltpu.make_async_remote_copy(
            src_ref=src, dst_ref=dst, send_sem=send, recv_sem=recv,
            device_id=peer, device_id_type=MESH,
        )

    def kept(q):
        return pl.ds(pl.multiple_of(q * quarter, quarter), quarter)

    def held(which, q):
        start = (q // 2) * half + which * run + lax.rem(q, 2) * quarter
        return pl.ds(pl.multiple_of(start, quarter), quarter)

    def piece(ctx, at):
        return weights.at[:, pl.ds(pl.multiple_of((ctx * 2 + at) * depth, depth), depth)]

    barrier = pltpu.get_barrier_semaphore()
    others = [at_clu(lax.rem(c + d, owners)) for d in range(1, owners)]
    others += [core_peer, y_peer, x_peer]
    for peer in others:
        pl.semaphore_signal(barrier, inc=1, device_id=peer, device_id_type=MESH)
    local = [
        pltpu.make_async_copy(
            tok_ref.at[:, pl.ds(pl.multiple_of(i * half + pair * run, run), run)],
            rows.at[c, :, pl.ds(i * run, run)], own_sem.at[i],
        )
        for i in range(2)
    ]
    local.append(pltpu.make_async_copy(w_ref.at[side], piece(a, side), own_sem.at[2]))
    local.append(pltpu.make_async_copy(cl_ref.at[c], ids.at[c], own_sem.at[3]))
    for copy in local:
        copy.start()
    pl.semaphore_wait(barrier, len(others))

    blocks = [
        (1 - pair) * 2 + pair,
        (1 - pair) * 2 + 1 - pair,
        mate,
    ]

    def cross():
        turn = jnp.where(near, 0, 1)
        return remote(
            tok_ref.at[:, held(1 - pair, t)], rows.at[c, :, kept(t)],
            cross_send.at[0], cross_recv.at[turn], at_clu(2 - pair),
        )

    def cross_came(n):
        here = rows.at[blocks[n], :, kept(t)]
        return remote(here, here, cross_send.at[0], cross_recv.at[n], at_clu(mate))

    def forward(n):
        here = rows.at[blocks[n], :, kept(t)]
        return remote(here, here, fwd_send.at[n], fwd_recv.at[n], at_clu(mate))

    def to_mate():
        return remote(
            tok_ref.at[:, held(pair, t)], rows.at[c, :, kept(t)],
            mate_send.at[0], mate_recv.at[0], at_clu(mate),
        )

    def mate_came():
        here = rows.at[mate, :, kept(t)]
        return remote(here, here, mate_send.at[0], mate_recv.at[0], at_clu(mate))

    def shared(n, q, send, recv, peer):
        here = rows.at[blocks[n], :, kept(q)]
        return remote(here, here, send.at[n], recv.at[n], peer)

    def to_core(n, q):
        return shared(n, q, core_send, core_recv, core_peer)

    def to_y(n, q):
        return shared(n, q, y_send, y_recv, y_peer)

    def to_core_far(n, q):
        return shared(n, q, far_send, far_recv, core_peer)

    def w_mate():
        return remote(w_ref.at[1 - side], piece(a, side), wm_send.at[0], wm_recv.at[0], at_clu(mate))

    def w_mate_came():
        here = piece(a, 1 - side)
        return remote(here, here, wm_send.at[0], wm_recv.at[0], at_clu(mate))

    def w_cross(i, ctx):
        here = piece(ctx, side if i == 0 else 1 - side)
        return remote(w_ref.at[side] if i == 0 else here, here, wx_send.at[i], wx_recv.at[i], x_peer)

    def id_hop(d):
        goal = lax.rem(c + d, owners)
        return remote(cl_ref.at[goal], ids.at[c], id_send.at[d - 1], id_recv.at[d - 1], at_clu(goal))

    def id_came(d):
        source = lax.rem(c + owners - d, owners)
        return remote(ids.at[source], ids.at[source], id_send.at[d - 1], id_recv.at[d - 1], at_clu(source))

    def part_hop(block):
        return remote(part.at[block], theirs.at[block], part_send.at[block], part_recv.at[block], at_clu(twin))

    cross().start()
    w_cross(0, a).start()
    w_mate().start()
    to_mate().start()
    for d in range(1, owners):
        id_hop(d).start()

    def share(n):
        to_y(n, t).start()
        to_core(n, t).start()

    def relay(n):
        q = (1 - y) * 2 + k
        to_y(n, q).wait_recv()
        to_core_far(n, q).start()

    def arrive_near(n):
        cross_came(n).wait_recv()
        forward(n).start()
        share(n)

    def arrive_far(n):
        forward(n).wait_recv()
        share(n)

    def project(block):
        held_rows = rows[block]
        given = jnp.dot(held_rows, weights[1 - pair], preferred_element_type=jnp.float32)
        part[block] = given.astype(jnp.bfloat16)
        part_hop(block).start()
        mine[block] = jnp.dot(held_rows, weights[pair], preferred_element_type=jnp.float32)

    def finish(n):
        to_core(n, y * 2 + 1 - k).wait_recv()
        to_core_far(n, (1 - y) * 2 + 1 - k).wait_recv()
        project(blocks[n])

    pl.when(near)(lambda: arrive_near(0))
    w_mate_came().wait_recv()
    w_cross(1, a).start()
    mate_came().wait_recv()
    share(2)
    pl.when(jnp.logical_not(near))(lambda: arrive_far(0))
    pl.when(near)(lambda: arrive_near(1))
    relay(2)
    for copy in local:
        copy.wait()
    for i in range(2):
        w_cross(i, 1 - a).wait_recv()
    project(c)
    finish(2)
    relay(0)
    pl.when(jnp.logical_not(near))(lambda: arrive_far(1))
    finish(0)
    relay(1)
    finish(1)
    for d in range(1, owners):
        id_came(d).wait_recv()
    for block in range(owners):
        part_hop(block).wait_recv()
        proj[block] = (mine[block] + theirs[block].astype(jnp.float32)).astype(jnp.bfloat16)

    def send_reply(goal):
        return remote(
            reply.at[goal], out_ref.at[:, pl.ds(pl.multiple_of(c * head_dim, head_dim), head_dim)],
            out_send.at[goal], out_recv.at[c], at_clu(goal),
        )

    def keep_reply(goal):
        return pltpu.make_async_copy(
            reply.at[goal], out_ref.at[:, pl.ds(pl.multiple_of(c * head_dim, head_dim), head_dim)],
            out_send.at[goal],
        )

    for goal in reversed(range(owners)):
        query = proj[goal, :, :head_dim]
        query_ids = jnp.transpose(ids[goal])[:, :1]
        parts = []
        for block in range(goal + 1):
            scores = lax.dot_general(
                query, proj[block, :, :head_dim], (((1,), (1,)), ((), ())),
                preferred_element_type=jnp.float32,
            ) * score_scale
            admitted = query_ids == ids[block, :1, :]
            if block == goal:
                at = lax.broadcasted_iota(jnp.int32, (count, count), 0)
                to = lax.broadcasted_iota(jnp.int32, (count, count), 1)
                scores = jnp.where(at == to, -100000.0, scores)
                admitted = admitted & (to <= at)
            parts.append(jnp.where(admitted, scores, -1e30))
        top = functools.reduce(jnp.maximum, [jnp.max(p, axis=1, keepdims=True) for p in parts])
        total = jnp.zeros((count, 1), jnp.float32)
        mixed = jnp.zeros((count, head_dim), jnp.float32)
        for block, piece_scores in enumerate(parts):
            weighed = jnp.exp(piece_scores - top)
            total += jnp.sum(weighed, axis=1, keepdims=True)
            mixed += jnp.dot(
                weighed.astype(jnp.bfloat16), proj[block, :, head_dim:],
                preferred_element_type=jnp.float32,
            )
        reply[goal] = (mixed / total).astype(jnp.bfloat16)
        pl.when(c != goal)(lambda goal=goal: send_reply(goal).start())
        pl.when(c == goal)(lambda goal=goal: keep_reply(goal).start())

    cross().wait_send()
    w_mate().wait_send()
    to_mate().wait_send()
    for i in range(2):
        w_cross(i, a).wait_send()
    for d in range(1, owners):
        id_hop(d).wait_send()
    for n in range(2):
        pl.when(near)(lambda n=n: forward(n).wait_send())
    for n in range(3):
        to_y(n, t).wait_send()
        to_core(n, t).wait_send()
        to_core_far(n, (1 - y) * 2 + k).wait_send()
    for block in range(owners):
        part_hop(block).wait_send()
    for goal in range(owners):
        @pl.when(c != goal)
        def _(goal=goal):
            send_reply(goal).wait_send()
            column = out_ref.at[:, pl.ds(goal * head_dim, head_dim)]
            remote(reply.at[goal], column, out_send.at[goal], out_recv.at[goal], at_clu(goal)).wait_recv()

        pl.when(c == goal)(lambda goal=goal: keep_reply(goal).wait())


def head_body(tokens, proj_weight, clusters):
    row_count, width = tokens.shape[1:]
    owners = lax.axis_size("clu")
    heads_here = clusters.shape[2]
    depth, _, proj_width = proj_weight.shape
    head_dim = proj_width // heads_here
    pieces = (
        proj_weight.reshape(depth, 2, 2, 2, head_dim)
        .transpose(3, 2, 0, 1, 4)
        .reshape(2, 2, depth, 2 * head_dim)
    )
    labels = jnp.broadcast_to(clusters[0].T[:, None, :], (heads_here, 8, row_count))
    steps = owners - 1
    dma = pltpu.SemaphoreType.DMA
    block = (owners, row_count, 2 * head_dim)
    out = pl.pallas_call(
        functools.partial(head_kernel, owners, depth, head_dim, head_dim ** (-0.5)),
        out_shape=jax.ShapeDtypeStruct((row_count, proj_width), jnp.bfloat16),
        in_specs=[pl.BlockSpec(memory_space=pl.ANY)] * 3,
        out_specs=pl.BlockSpec(memory_space=pl.ANY),
        scratch_shapes=[
            pltpu.VMEM((owners, row_count, width // 2), jnp.bfloat16),
            pltpu.VMEM((2, width // 2, 2 * head_dim), jnp.bfloat16),
            pltpu.VMEM((owners, 8, row_count), jnp.int32),
            pltpu.VMEM(block, jnp.float32),
            pltpu.VMEM(block, jnp.bfloat16),
            pltpu.VMEM(block, jnp.bfloat16),
            pltpu.VMEM(block, jnp.bfloat16),
            pltpu.VMEM((owners, row_count, head_dim), jnp.bfloat16),
            dma((4,)),
            dma((1,)), dma((1,)),
            dma((2,)), dma((2,)),
            dma((steps,)), dma((steps,)),
            dma((1,)), dma((2,)),
            dma((2,)), dma((2,)),
            dma((1,)), dma((1,)),
            dma((3,)), dma((3,)),
            dma((3,)), dma((3,)),
            dma((3,)), dma((3,)),
            dma((owners,)), dma((owners,)),
            dma((owners,)), dma((owners,)),
        ],
        compiler_params=pltpu.CompilerParams(
            collective_id=0, has_side_effects=True, vmem_limit_bytes=56 * 1024 * 1024
        ),
    )(tokens[0], pieces, labels)
    return out[None]


def body(tokens, proj_weight, clusters):
    local_rows = tokens[0]
    row_count = local_rows.shape[0]
    owners = lax.axis_size("clu")
    heads_here = clusters.shape[2]
    proj_width = proj_weight.shape[2]
    head_dim = proj_width // heads_here
    capacity = 2 * row_count // owners
    per_owner = CLUSTERS // owners
    length = row_count * owners
    total_slots = owners * capacity
    score_scale = head_dim ** (-0.5)
    weight_piece = lax.all_gather(proj_weight, ("ctx", "clu"), axis=0, tiled=True)
    flat_piece = weight_piece.reshape(weight_piece.shape[0], 2 * proj_width)
    summed = jnp.dot(local_rows, flat_piece, preferred_element_type=jnp.float32)
    projected = summed.astype(jnp.bfloat16)
    queries = projected[:, :proj_width].reshape(row_count, heads_here, head_dim)
    values = projected[:, proj_width:].reshape(row_count, heads_here, head_dim)
    features = jnp.concatenate([queries, values], axis=2).transpose(1, 0, 2)
    cluster_ids = clusters[0]
    owner_of = cluster_ids // per_owner
    onehot = (owner_of[:, :, None] == jnp.arange(owners, dtype=jnp.int32)[None, None, :]).astype(
        jnp.int32
    )
    rank_in = jnp.sum((jnp.cumsum(onehot, axis=0) - onehot) * onehot, axis=2)
    slot_of = (owner_of * capacity + rank_in).T
    head_rows = jnp.arange(heads_here, dtype=jnp.int32)[:, None]
    token_index = jnp.broadcast_to(
        jnp.arange(row_count, dtype=jnp.int32)[None, :], (heads_here, row_count)
    )
    source = jnp.zeros((heads_here, total_slots), jnp.int32).at[head_rows, slot_of].set(token_index)
    positions = lax.axis_index("clu") * row_count + jnp.arange(row_count, dtype=jnp.int32)
    labels = cluster_ids.T * length + positions[None, :]
    slot_tags = (
        jnp.full((heads_here, total_slots), -1, jnp.int32).at[head_rows, slot_of].set(labels)
    )
    outgoing = jnp.take_along_axis(features, source[:, :, None], axis=1)
    outgoing = jnp.where((slot_tags >= 0)[:, :, None], outgoing, jnp.zeros_like(outgoing))
    outgoing = outgoing.reshape(heads_here, owners, capacity, 2 * head_dim)
    slot_tags = slot_tags.reshape(heads_here, owners, capacity)

    def attend_head(head_item):
        slot_block, key_tags = head_item
        flattened = slot_block.reshape(-1, 2 * head_dim)
        key_rows = flattened[:, :head_dim]
        value_rows = flattened[:, head_dim:]
        key_tags = key_tags.reshape(-1)
        scores = (
            jnp.einsum("qd,kd->qk", key_rows, key_rows, preferred_element_type=jnp.float32)
            * score_scale
        )
        tag_group = key_tags // length
        tag_pos = key_tags % length
        admitted = (
            (key_tags[None, :] >= 0)
            & (tag_group[None, :] == tag_group[:, None])
            & (tag_pos[None, :] <= tag_pos[:, None])
        )
        scores = jnp.where(key_tags[None, :] == key_tags[:, None], -100000.0, scores)
        scores = jnp.where(admitted, scores, -1e30)
        row_max = jnp.max(scores, axis=1, keepdims=True)
        exp_scores = jnp.exp(scores - row_max)
        row_total = jnp.sum(exp_scores, axis=1, keepdims=True)
        probabilities = (exp_scores / row_total).astype(jnp.bfloat16)
        result = jnp.dot(probabilities, value_rows, preferred_element_type=jnp.float32).astype(
            jnp.bfloat16
        )
        return result.reshape(slot_block.shape[0], slot_block.shape[1], head_dim)

    replies = lax.map(
        attend_head,
        (
            lax.all_to_all(outgoing, "clu", split_axis=1, concat_axis=1, tiled=True),
            lax.all_to_all(slot_tags, "clu", split_axis=1, concat_axis=1, tiled=True),
        ),
    )
    returned = lax.all_to_all(replies, "clu", split_axis=1, concat_axis=1, tiled=True)
    returned = returned.reshape(heads_here, total_slots, head_dim)
    gathered = jnp.take_along_axis(returned, slot_of[:, :, None], axis=1)
    return gathered.transpose(1, 0, 2).reshape(1, row_count, heads_here * head_dim)


def solution(mesh):
    sizes = dict(mesh.shape)
    heads_here = 16 // sizes["tp"]
    by_head = sizes["ctx"] == 2 and sizes["tp"] == 4 and sizes["clu"] == heads_here == 4
    return jax.shard_map(
        head_body if by_head else body,
        mesh=mesh,
        in_specs=(P("ctx", "clu", None), P(("ctx", "clu"), None, "tp"), P("ctx", "clu", "tp")),
        out_specs=P("ctx", "clu", "tp"),
        check_vma=False,
    )
```

time: 90.9 us -> 71.3 us (0.78)
  Pallas kernels: 85.1 us -> 64.7 us
  local copies, waits for them, and re-layouts: 4.95 us -> 6.34 us
    pallas_call x1, Pallas kernels: 85.1 us -> 64.7 us  [head_body(): pl.pallas_call(functools.partial(head_kernel, owners, depth, head_dim, he...]
    reshape x1 -> x3, local copies, waits for them, and re-layouts: 0.71 us -> 4.05 us  [the longest x2 2.54 us: head_body(): proj_weight.reshape(depth, 2, 2, 2, head_dim).transpose(3, 2, 0, 1, 4)]
    unnamed x7 -> x3, local copies, waits for them, and re-layouts: 3.52 us -> 1.68 us
where the time goes in v2:
time: 71.3 us; the launch traced here: 71.1 us
  Pallas kernels  64.7 us (91%)
  local copies, waits for them, and re-layouts  6.34 us (9%)
    pallas_call x1, Pallas kernels, head_body(): pl.pallas_call(functools.partial(head_kernel, owners, depth, head_dim, he...  64.7 us
    reshape x2, local copies, waits for them, and re-layouts, head_body(): proj_weight.reshape(depth, 2, 2, 2, head_dim).transpose(3, 2, 0, 1, 4)  2.54 us
    unnamed x3, local copies, waits for them, and re-layouts  1.68 us
    reshape x1, local copies, waits for them, and re-layouts, head_body(): pieces = proj_weight.reshape(depth, 2, 2, 2, head_dim).transpose(3, 2, 0,...  1.51 us

profile of v2, /device:TPU:0, one launch (start us, length us, event | category | flops | bytes accessed | tf_op | source)
XLA Modules:
  0.0 71.1 jit_solution(12674401689803587220)
XLA Ops:
  0.0 1.7 %reshape.7 = bf16[512,2,2,2,128]{4,3,2,1,0:T(2,128)(2,1)S(1)} reshape(bf16[512,2,512]{2,1,0:T(2,128)(2,1)} %param.4) | data formatting | bytes 2097152 | tf_op jit(solution)/shard_map/reshape | solution.py:280
  1.7 0.0 copy-start
  1.8 0.8 %copy.6 = bf16[512,2,2,2,128]{4,1,0,2,3:T(2,128)(2,1)S(1)} copy(bf16[512,2,2,2,128]{4,3,2,1,0:T(2,128)(2,1)S(1)} %reshape.7) | data formatting | bytes 2097152 | tf_op jit(solution)/shard_map/reshape | solution.py:280
  2.6 1.5 %reshape.8.w_ref = bf16[2,2,512,256]{3,2,1,0:T(8,128)(2,1)} reshape(bf16[2,2,512,2,128]{4,3,2,1,0:T(2,128)(2,1)S(1)} %bitcast.8) | data formatting | bytes 2097152 | tf_op jit(solution)/shard_map/reshape | solution.py:282
  4.1 0.0 copy-done
  4.1 0.6 broadcast_in_dim.4.cl_ref
  4.7 64.7 %shard_map.37 = bf16[256,512]{1,0:T(8,128)(2,1)} custom-call(bf16[256,4096]{1,0:T(8,128)(2,1)} %bitcast.9, bf16[2,2,512,256]{3,2,1,0:T(8,128)(2,1)} %reshape.8.w_ref, s32[4,8,256]{2,1,0:T(8,128)} %broadcast_in_dim.4.cl_ref), custom_call_target="tpu_custom_call" | custom-call | tf_op jit(solution)/shard_map/pallas_call | solution.py:288
  69.4 1.7 %copy.8 = bf16[1,256,512]{2,1,0:T(8,128)(2,1)} copy(bf16[1,256,512]{2,1,0:T(8,128)(2,1)} %bitcast.10) | data formatting | bytes 524288
Async XLA Ops:
  1.7 2.3 %copy-start = (s32[1,256,4]{1,2,0:T(4,128)S(1)}, s32[1,256,4]{1,2,0:T(4,128)}, u32[]{:S(2)}) copy-start(s32[1,256,4]{1,2,0:T(4,128)} %param.5) | copy-start | bytes 12292

commit v3 on v2

--- a/solution.py
+++ b/solution.py
@@ -54,8 +54,21 @@
         start = (q // 2) * half + which * run + lax.rem(q, 2) * quarter
         return pl.ds(pl.multiple_of(start, quarter), quarter)
 
-    def piece(ctx, at):
-        return weights.at[:, pl.ds(pl.multiple_of((ctx * 2 + at) * depth, depth), depth)]
+    heads = (1 - pair, pair)
+
+    def piece(ctx, at, role):
+        return weights.at[heads[role], pl.ds(pl.multiple_of((ctx * 2 + at) * depth, depth), depth)]
+
+    def spread(at, role):
+        start = pl.multiple_of((heads[role] * 2 + at) * head_dim, head_dim)
+        lands = pl.multiple_of((a * 2 + side) * depth, depth)
+        return [
+            (
+                w_ref.at[kind, :, pl.ds(start, head_dim)],
+                weights.at[heads[role], pl.ds(lands, depth), pl.ds(kind * head_dim, head_dim)],
+            )
+            for kind in range(2)
+        ]
 
     barrier = pltpu.get_barrier_semaphore()
     others = [at_clu(lax.rem(c + d, owners)) for d in range(1, owners)]
@@ -69,10 +82,12 @@
         )
         for i in range(2)
     ]
-    local.append(pltpu.make_async_copy(w_ref.at[side], piece(a, side), own_sem.at[2]))
-    local.append(pltpu.make_async_copy(cl_ref.at[c], ids.at[c], own_sem.at[3]))
+    local.append(pltpu.make_async_copy(cl_ref.at[c], ids.at[c], own_sem.at[2]))
     for copy in local:
         copy.start()
+    for role in range(2):
+        for src, dst in spread(side, role):
+            pltpu.make_async_copy(src, dst, own_sem.at[3 + role]).start()
     pl.semaphore_wait(barrier, len(others))
 
     blocks = [
@@ -119,16 +134,31 @@
     def to_core_far(n, q):
         return shared(n, q, far_send, far_recv, core_peer)
 
-    def w_mate():
-        return remote(w_ref.at[1 - side], piece(a, side), wm_send.at[0], wm_recv.at[0], at_clu(mate))
-
-    def w_mate_came():
-        here = piece(a, 1 - side)
-        return remote(here, here, wm_send.at[0], wm_recv.at[0], at_clu(mate))
-
-    def w_cross(i, ctx):
-        here = piece(ctx, side if i == 0 else 1 - side)
-        return remote(w_ref.at[side] if i == 0 else here, here, wx_send.at[i], wx_recv.at[i], x_peer)
+    def w_mate(role):
+        for src, dst in spread(1 - side, role):
+            remote(src, dst, wm_send.at[role], wm_recv.at[role], at_clu(mate)).start()
+
+    def w_mate_all(role):
+        here = piece(a, 1 - side, role)
+        return remote(here, here, wm_send.at[role], wm_recv.at[role], at_clu(mate))
+
+    def w_cross_own(role):
+        for src, dst in spread(side, role):
+            remote(src, dst, wx_send.at[0, role], wx_recv.at[0, role], x_peer).start()
+
+    def w_cross(i, ctx, role):
+        here = piece(ctx, side if i == 0 else 1 - side, role)
+        return remote(here, here, wx_send.at[i, role], wx_recv.at[i, role], x_peer)
+
+    def w_pass(role):
+        w_mate_all(role).wait_recv()
+        w_cross(1, a, role).start()
+
+    def w_ready(role):
+        here = piece(a, side, role)
+        pltpu.make_async_copy(here, here, own_sem.at[3 + role]).wait()
+        for i in range(2):
+            w_cross(i, 1 - a, role).wait_recv()
 
     def id_hop(d):
         goal = lax.rem(c + d, owners)
@@ -142,9 +172,11 @@
         return remote(part.at[block], theirs.at[block], part_send.at[block], part_recv.at[block], at_clu(twin))
 
     cross().start()
-    w_cross(0, a).start()
-    w_mate().start()
+    w_cross_own(0)
+    w_mate(0)
     to_mate().start()
+    w_cross_own(1)
+    pl.when(jnp.logical_not(near))(lambda: w_mate(1))
     for d in range(1, owners):
         id_hop(d).start()
 
@@ -166,37 +198,42 @@
         forward(n).wait_recv()
         share(n)
 
-    def project(block):
-        held_rows = rows[block]
-        given = jnp.dot(held_rows, weights[1 - pair], preferred_element_type=jnp.float32)
+    def give(block):
+        given = jnp.dot(rows[block], weights[1 - pair], preferred_element_type=jnp.float32)
         part[block] = given.astype(jnp.bfloat16)
         part_hop(block).start()
-        mine[block] = jnp.dot(held_rows, weights[pair], preferred_element_type=jnp.float32)
 
     def finish(n):
         to_core(n, y * 2 + 1 - k).wait_recv()
         to_core_far(n, (1 - y) * 2 + 1 - k).wait_recv()
-        project(blocks[n])
+        give(blocks[n])
 
     pl.when(near)(lambda: arrive_near(0))
-    w_mate_came().wait_recv()
-    w_cross(1, a).start()
+    w_pass(0)
+
+    @pl.when(near)
+    def _():
+        arrive_near(1)
+        w_mate(1)
+
     mate_came().wait_recv()
     share(2)
     pl.when(jnp.logical_not(near))(lambda: arrive_far(0))
-    pl.when(near)(lambda: arrive_near(1))
     relay(2)
     for copy in local:
         copy.wait()
-    for i in range(2):
-        w_cross(i, 1 - a).wait_recv()
-    project(c)
+    w_ready(0)
+    give(c)
     finish(2)
     relay(0)
     pl.when(jnp.logical_not(near))(lambda: arrive_far(1))
+    w_pass(1)
     finish(0)
     relay(1)
     finish(1)
+    w_ready(1)
+    for block in range(owners):
+        mine[block] = jnp.dot(rows[block], weights[pair], preferred_element_type=jnp.float32)
     for d in range(1, owners):
         id_came(d).wait_recv()
     for block in range(owners):
@@ -246,10 +283,11 @@
         pl.when(c == goal)(lambda goal=goal: keep_reply(goal).start())
 
     cross().wait_send()
-    w_mate().wait_send()
     to_mate().wait_send()
-    for i in range(2):
-        w_cross(i, a).wait_send()
+    for role in range(2):
+        w_mate_all(role).wait_send()
+        for i in range(2):
+            w_cross(i, a, role).wait_send()
     for d in range(1, owners):
         id_hop(d).wait_send()
     for n in range(2):
@@ -276,11 +314,7 @@
     heads_here = clusters.shape[2]
     depth, _, proj_width = proj_weight.shape
     head_dim = proj_width // heads_here
-    pieces = (
-        proj_weight.reshape(depth, 2, 2, 2, head_dim)
-        .transpose(3, 2, 0, 1, 4)
-        .reshape(2, 2, depth, 2 * head_dim)
-    )
+    kinds = proj_weight.transpose(1, 0, 2)
     labels = jnp.broadcast_to(clusters[0].T[:, None, :], (heads_here, 8, row_count))
     steps = owners - 1
     dma = pltpu.SemaphoreType.DMA
@@ -288,7 +322,7 @@
     out = pl.pallas_call(
         functools.partial(head_kernel, owners, depth, head_dim, head_dim ** (-0.5)),
         out_shape=jax.ShapeDtypeStruct((row_count, proj_width), jnp.bfloat16),
-        in_specs=[pl.BlockSpec(memory_space=pl.ANY)] * 3,
+        in_specs=[pl.BlockSpec(memory_space=space) for space in (pltpu.HBM, pl.ANY, pl.ANY)],
         out_specs=pl.BlockSpec(memory_space=pl.ANY),
         scratch_shapes=[
             pltpu.VMEM((owners, row_count, width // 2), jnp.bfloat16),
@@ -299,9 +333,9 @@
             pltpu.VMEM(block, jnp.bfloat16),
             pltpu.VMEM(block, jnp.bfloat16),
             pltpu.VMEM((owners, row_count, head_dim), jnp.bfloat16),
-            dma((4,)),
-            dma((1,)), dma((1,)),
+            dma((5,)),
             dma((2,)), dma((2,)),
+            dma((2, 2)), dma((2, 2)),
             dma((steps,)), dma((steps,)),
             dma((1,)), dma((2,)),
             dma((2,)), dma((2,)),
@@ -313,9 +347,9 @@
             dma((owners,)), dma((owners,)),
         ],
         compiler_params=pltpu.CompilerParams(
-            collective_id=0, has_side_effects=True, vmem_limit_bytes=56 * 1024 * 1024
+            collective_id=0, has_side_effects=True, vmem_limit_bytes=40 * 1024 * 1024
         ),
-    )(tokens[0], pieces, labels)
+    )(tokens[0], kinds, labels)
     return out[None]
 
 

time: 71.3 us -> 65.2 us (0.914)
  local copies, waits for them, and re-layouts: 6.34 us -> 2.94 us
  Pallas kernels: 64.7 us -> 62.1 us
    reshape x3 -> x0, local copies, waits for them, and re-layouts: 4.05 us -> none  [the longest x2 2.54 us: head_body(): proj_weight.reshape(depth, 2, 2, 2, head_dim).transpose(3, 2, 0, 1, 4)]
    pallas_call x1, Pallas kernels: 64.7 us -> 62.1 us  [head_body(): pl.pallas_call(functools.partial(head_kernel, owners, depth, head_dim, he...]
    unnamed x3 -> x4, local copies, waits for them, and re-layouts: 1.68 us -> 2.1 us
where the time goes in v3:
time: 65.2 us; the launch traced here: 65.1 us
  Pallas kernels  62.1 us (95%)
  local copies, waits for them, and re-layouts  2.94 us (5%)
    pallas_call x1, Pallas kernels, head_body(): pl.pallas_call(functools.partial(head_kernel, owners, depth, head_dim, he...  62.1 us
    unnamed x4, local copies, waits for them, and re-layouts  2.1 us

profile of v3, /device:TPU:0, one launch (start us, length us, event | category | flops | bytes accessed | tf_op | source)
XLA Modules:
  0.0 65.1 jit_solution(4120851957189028565)
XLA Ops:
  0.0 0.0 copy-start
  0.0 0.8 %broadcast_in_dim.4.cl_ref = s32[4,8,256]{2,1,0:T(8,128)S(1)} broadcast(s32[4,256]{1,0:T(4,128)} %bitcast.11), dimensions={0,2} | broadcast | bytes 36864 | tf_op jit(solution)/shard_map/broadcast_in_dim | solution.py:318
  0.8 1.4 %copy.6 = bf16[512,2,512]{2,0,1:T(8,128)(2,1)S(1)} copy(bf16[512,2,512]{2,1,0:T(2,128)(2,1)} %param.4) | data formatting | bytes 2097152 | tf_op args[1]
  2.2 0.0 copy-done
  2.2 62.1 %shard_map.37 = bf16[256,512]{1,0:T(8,128)(2,1)S(1)} custom-call(bf16[256,4096]{1,0:T(8,128)(2,1)S(1)} %bitcast.9, bf16[2,512,512]{2,1,0:T(8,128)(2,1)S(1)} %bitcast.8, s32[4,8,256]{2,1,0:T(8,128)S(1)} %broadcast_in_dim.4.cl_ref), custom_call_target="tpu_custom_call" | custom-call | tf_op jit(solution)/shard_map/pallas_call | solution.py:322
  64.4 0.7 %copy.8 = bf16[1,256,512]{2,1,0:T(8,128)(2,1)} copy(bf16[1,256,512]{2,1,0:T(8,128)(2,1)S(1)} %bitcast.10) | data formatting | bytes 524288
Async XLA Ops:
  0.0 2.2 %copy-start = (bf16[1,256,4096]{2,1,0:T(8,128)(2,1)S(1)}, bf16[1,256,4096]{2,1,0:T(8,128)(2,1)}, u32[]{:S(2)}) copy-start(bf16[1,256,4096]{2,1,0:T(8,128)(2,1)} %param.3) | copy-start | bytes 6291460

commit v4 on v3

--- a/solution.py
+++ b/solution.py
@@ -171,15 +171,6 @@
     def part_hop(block):
         return remote(part.at[block], theirs.at[block], part_send.at[block], part_recv.at[block], at_clu(twin))
 
-    cross().start()
-    w_cross_own(0)
-    w_mate(0)
-    to_mate().start()
-    w_cross_own(1)
-    pl.when(jnp.logical_not(near))(lambda: w_mate(1))
-    for d in range(1, owners):
-        id_hop(d).start()
-
     def share(n):
         to_y(n, t).start()
         to_core(n, t).start()
@@ -208,29 +199,59 @@
         to_core_far(n, (1 - y) * 2 + 1 - k).wait_recv()
         give(blocks[n])
 
-    pl.when(near)(lambda: arrive_near(0))
-    w_pass(0)
+    cross().start()
+    w_cross_own(0)
+    w_mate(0)
+    pl.when(near)(lambda: to_mate().start())
+    w_cross_own(1)
+    for d in range(1, owners):
+        id_hop(d).start()
+    for copy in local:
+        copy.wait()
 
     @pl.when(near)
     def _():
+        arrive_near(0)
+        w_pass(0)
         arrive_near(1)
+        relay(0)
+        mate_came().wait_recv()
+        share(2)
+        relay(1)
+        w_ready(0)
+        give(c)
+        finish(0)
+        finish(1)
+        for n in range(2):
+            forward(n).wait_send()
         w_mate(1)
-
-    mate_came().wait_recv()
-    share(2)
-    pl.when(jnp.logical_not(near))(lambda: arrive_far(0))
-    relay(2)
-    for copy in local:
-        copy.wait()
-    w_ready(0)
-    give(c)
-    finish(2)
-    relay(0)
-    pl.when(jnp.logical_not(near))(lambda: arrive_far(1))
-    w_pass(1)
-    finish(0)
-    relay(1)
-    finish(1)
+        w_pass(1)
+        relay(2)
+        finish(2)
+        cross().wait_send()
+        w_mate_all(0).wait_send()
+
+    @pl.when(jnp.logical_not(near))
+    def _():
+        cross().wait_send()
+        to_mate().start()
+        w_pass(0)
+        w_mate_all(0).wait_send()
+        w_mate(1)
+        mate_came().wait_recv()
+        share(2)
+        arrive_far(0)
+        relay(2)
+        w_ready(0)
+        give(c)
+        finish(2)
+        arrive_far(1)
+        relay(0)
+        finish(0)
+        w_pass(1)
+        relay(1)
+        finish(1)
+
     w_ready(1)
     for block in range(owners):
         mine[block] = jnp.dot(rows[block], weights[pair], preferred_element_type=jnp.float32)
@@ -282,16 +303,13 @@
         pl.when(c != goal)(lambda goal=goal: send_reply(goal).start())
         pl.when(c == goal)(lambda goal=goal: keep_reply(goal).start())
 
-    cross().wait_send()
     to_mate().wait_send()
+    w_mate_all(1).wait_send()
     for role in range(2):
-        w_mate_all(role).wait_send()
         for i in range(2):
             w_cross(i, a, role).wait_send()
     for d in range(1, owners):
         id_hop(d).wait_send()
-    for n in range(2):
-        pl.when(near)(lambda n=n: forward(n).wait_send())
     for n in range(3):
         to_y(n, t).wait_send()
         to_core(n, t).wait_send()

time: 65.2 us -> 73.6 us (1.13)
  Pallas kernels: 62.1 us -> 70.5 us
    pallas_call x1, Pallas kernels: 62.1 us -> 70.5 us  [head_body(): pl.pallas_call(functools.partial(head_kernel, owners, depth, head_dim, he...]
where the time goes in v4:
time: 73.6 us; the launch traced here: 73.5 us
  Pallas kernels  70.5 us (96%)
  local copies, waits for them, and re-layouts  2.94 us (4%)
    pallas_call x1, Pallas kernels, head_body(): pl.pallas_call(functools.partial(head_kernel, owners, depth, head_dim, he...  70.5 us
    unnamed x4, local copies, waits for them, and re-layouts  2.1 us

profile of v4, /device:TPU:0, one launch (start us, length us, event | category | flops | bytes accessed | tf_op | source)
XLA Modules:
  0.0 73.5 jit_solution(8262594301069928542)
XLA Ops:
  0.0 0.0 copy-start
  0.0 0.8 %broadcast_in_dim.4.cl_ref = s32[4,8,256]{2,1,0:T(8,128)S(1)} broadcast(s32[4,256]{1,0:T(4,128)} %bitcast.11), dimensions={0,2} | broadcast | bytes 36864 | tf_op jit(solution)/shard_map/broadcast_in_dim | solution.py:336
  0.8 1.4 %copy.6 = bf16[512,2,512]{2,0,1:T(8,128)(2,1)S(1)} copy(bf16[512,2,512]{2,1,0:T(2,128)(2,1)} %param.4) | data formatting | bytes 2097152 | tf_op args[1]
  2.2 0.0 copy-done
  2.2 70.5 %shard_map.37 = bf16[256,512]{1,0:T(8,128)(2,1)S(1)} custom-call(bf16[256,4096]{1,0:T(8,128)(2,1)S(1)} %bitcast.9, bf16[2,512,512]{2,1,0:T(8,128)(2,1)S(1)} %bitcast.8, s32[4,8,256]{2,1,0:T(8,128)S(1)} %broadcast_in_dim.4.cl_ref), custom_call_target="tpu_custom_call" | custom-call | tf_op jit(solution)/shard_map/pallas_call | solution.py:340
  72.8 0.7 copy.8
Async XLA Ops:
  0.0 2.2 %copy-start = (bf16[1,256,4096]{2,1,0:T(8,128)(2,1)S(1)}, bf16[1,256,4096]{2,1,0:T(8,128)(2,1)}, u32[]{:S(2)}) copy-start(bf16[1,256,4096]{2,1,0:T(8,128)(2,1)} %param.3) | copy-start | bytes 6291460

commit v5 on v3

--- a/solution.py
+++ b/solution.py
@@ -14,7 +14,7 @@
 def head_kernel(
     owners, depth, head_dim, score_scale,
     tok_ref, w_ref, cl_ref, out_ref,
-    rows, weights, ids, mine, part, theirs, proj, reply,
+    rows, weights, stage, ids, mine, part, theirs, proj, reply,
     own_sem, wm_send, wm_recv, wx_send, wx_recv, id_send, id_recv,
     cross_send, cross_recv, fwd_send, fwd_recv, mate_send, mate_recv,
     core_send, core_recv, y_send, y_recv, far_send, far_recv,
@@ -47,9 +47,6 @@
             device_id=peer, device_id_type=MESH,
         )
 
-    def kept(q):
-        return pl.ds(pl.multiple_of(q * quarter, quarter), quarter)
-
     def held(which, q):
         start = (q // 2) * half + which * run + lax.rem(q, 2) * quarter
         return pl.ds(pl.multiple_of(start, quarter), quarter)
@@ -58,17 +55,6 @@
 
     def piece(ctx, at, role):
         return weights.at[heads[role], pl.ds(pl.multiple_of((ctx * 2 + at) * depth, depth), depth)]
-
-    def spread(at, role):
-        start = pl.multiple_of((heads[role] * 2 + at) * head_dim, head_dim)
-        lands = pl.multiple_of((a * 2 + side) * depth, depth)
-        return [
-            (
-                w_ref.at[kind, :, pl.ds(start, head_dim)],
-                weights.at[heads[role], pl.ds(lands, depth), pl.ds(kind * head_dim, head_dim)],
-            )
-            for kind in range(2)
-        ]
 
     barrier = pltpu.get_barrier_semaphore()
     others = [at_clu(lax.rem(c + d, owners)) for d in range(1, owners)]
@@ -76,18 +62,20 @@
     for peer in others:
         pl.semaphore_signal(barrier, inc=1, device_id=peer, device_id_type=MESH)
     local = [
-        pltpu.make_async_copy(
-            tok_ref.at[:, pl.ds(pl.multiple_of(i * half + pair * run, run), run)],
-            rows.at[c, :, pl.ds(i * run, run)], own_sem.at[i],
-        )
-        for i in range(2)
+        pltpu.make_async_copy(tok_ref.at[:, held(pair, q)], rows.at[c, q], own_sem.at[q])
+        for q in range(4)
     ]
-    local.append(pltpu.make_async_copy(cl_ref.at[c], ids.at[c], own_sem.at[2]))
+    local.append(pltpu.make_async_copy(cl_ref.at[c], ids.at[c], own_sem.at[4]))
     for copy in local:
         copy.start()
     for role in range(2):
-        for src, dst in spread(side, role):
-            pltpu.make_async_copy(src, dst, own_sem.at[3 + role]).start()
+        for kind in range(2):
+            lands = pl.ds(kind * head_dim, head_dim)
+            start = pl.multiple_of((heads[role] * 2 + side) * head_dim, head_dim)
+            mine_at = pl.ds(pl.multiple_of((a * 2 + side) * depth, depth), depth)
+            weights[heads[role], mine_at, lands] = w_ref[kind, :, pl.ds(start, head_dim)]
+            start = pl.multiple_of((heads[role] * 2 + 1 - side) * head_dim, head_dim)
+            stage[role, :, lands] = w_ref[kind, :, pl.ds(start, head_dim)]
     pl.semaphore_wait(barrier, len(others))
 
     blocks = [
@@ -99,30 +87,30 @@
     def cross():
         turn = jnp.where(near, 0, 1)
         return remote(
-            tok_ref.at[:, held(1 - pair, t)], rows.at[c, :, kept(t)],
+            tok_ref.at[:, held(1 - pair, t)], rows.at[c, t],
             cross_send.at[0], cross_recv.at[turn], at_clu(2 - pair),
         )
 
     def cross_came(n):
-        here = rows.at[blocks[n], :, kept(t)]
+        here = rows.at[blocks[n], t]
         return remote(here, here, cross_send.at[0], cross_recv.at[n], at_clu(mate))
 
     def forward(n):
-        here = rows.at[blocks[n], :, kept(t)]
+        here = rows.at[blocks[n], t]
         return remote(here, here, fwd_send.at[n], fwd_recv.at[n], at_clu(mate))
 
     def to_mate():
         return remote(
-            tok_ref.at[:, held(pair, t)], rows.at[c, :, kept(t)],
+            tok_ref.at[:, held(pair, t)], rows.at[c, t],
             mate_send.at[0], mate_recv.at[0], at_clu(mate),
         )
 
     def mate_came():
-        here = rows.at[mate, :, kept(t)]
+        here = rows.at[mate, t]
         return remote(here, here, mate_send.at[0], mate_recv.at[0], at_clu(mate))
 
     def shared(n, q, send, recv, peer):
-        here = rows.at[blocks[n], :, kept(q)]
+        here = rows.at[blocks[n], q]
         return remote(here, here, send.at[n], recv.at[n], peer)
 
     def to_core(n, q):
@@ -135,28 +123,23 @@
         return shared(n, q, far_send, far_recv, core_peer)
 
     def w_mate(role):
-        for src, dst in spread(1 - side, role):
-            remote(src, dst, wm_send.at[role], wm_recv.at[role], at_clu(mate)).start()
-
-    def w_mate_all(role):
+        return remote(
+            stage.at[role], piece(a, side, role), wm_send.at[role], wm_recv.at[role], at_clu(mate)
+        )
+
+    def w_mate_came(role):
         here = piece(a, 1 - side, role)
         return remote(here, here, wm_send.at[role], wm_recv.at[role], at_clu(mate))
-
-    def w_cross_own(role):
-        for src, dst in spread(side, role):
-            remote(src, dst, wx_send.at[0, role], wx_recv.at[0, role], x_peer).start()
 
     def w_cross(i, ctx, role):
         here = piece(ctx, side if i == 0 else 1 - side, role)
         return remote(here, here, wx_send.at[i, role], wx_recv.at[i, role], x_peer)
 
     def w_pass(role):
-        w_mate_all(role).wait_recv()
+        w_mate_came(role).wait_recv()
         w_cross(1, a, role).start()
 
     def w_ready(role):
-        here = piece(a, side, role)
-        pltpu.make_async_copy(here, here, own_sem.at[3 + role]).wait()
         for i in range(2):
             w_cross(i, 1 - a, role).wait_recv()
 
@@ -172,11 +155,11 @@
         return remote(part.at[block], theirs.at[block], part_send.at[block], part_recv.at[block], at_clu(twin))
 
     cross().start()
-    w_cross_own(0)
-    w_mate(0)
+    w_cross(0, a, 0).start()
+    w_mate(0).start()
     to_mate().start()
-    w_cross_own(1)
-    pl.when(jnp.logical_not(near))(lambda: w_mate(1))
+    w_cross(0, a, 1).start()
+    pl.when(jnp.logical_not(near))(lambda: w_mate(1).start())
     for d in range(1, owners):
         id_hop(d).start()
 
@@ -198,8 +181,11 @@
         forward(n).wait_recv()
         share(n)
 
+    def whole(block):
+        return jnp.concatenate([rows[block, q] for q in range(4)], axis=1)
+
     def give(block):
-        given = jnp.dot(rows[block], weights[1 - pair], preferred_element_type=jnp.float32)
+        given = jnp.dot(whole(block), weights[1 - pair], preferred_element_type=jnp.float32)
         part[block] = given.astype(jnp.bfloat16)
         part_hop(block).start()
 
@@ -214,7 +200,7 @@
     @pl.when(near)
     def _():
         arrive_near(1)
-        w_mate(1)
+        w_mate(1).start()
 
     mate_came().wait_recv()
     share(2)
@@ -233,7 +219,7 @@
     finish(1)
     w_ready(1)
     for block in range(owners):
-        mine[block] = jnp.dot(rows[block], weights[pair], preferred_element_type=jnp.float32)
+        mine[block] = jnp.dot(whole(block), weights[pair], preferred_element_type=jnp.float32)
     for d in range(1, owners):
         id_came(d).wait_recv()
     for block in range(owners):
@@ -285,7 +271,7 @@
     cross().wait_send()
     to_mate().wait_send()
     for role in range(2):
-        w_mate_all(role).wait_send()
+        w_mate(role).wait_send()
         for i in range(2):
             w_cross(i, a, role).wait_send()
     for d in range(1, owners):
@@ -322,11 +308,12 @@
     out = pl.pallas_call(
         functools.partial(head_kernel, owners, depth, head_dim, head_dim ** (-0.5)),
         out_shape=jax.ShapeDtypeStruct((row_count, proj_width), jnp.bfloat16),
-        in_specs=[pl.BlockSpec(memory_space=space) for space in (pltpu.HBM, pl.ANY, pl.ANY)],
+        in_specs=[pl.BlockSpec(memory_space=space) for space in (pl.ANY, pltpu.VMEM, pl.ANY)],
         out_specs=pl.BlockSpec(memory_space=pl.ANY),
         scratch_shapes=[
-            pltpu.VMEM((owners, row_count, width // 2), jnp.bfloat16),
+            pltpu.VMEM((owners, 4, row_count, width // 8), jnp.bfloat16),
             pltpu.VMEM((2, width // 2, 2 * head_dim), jnp.bfloat16),
+            pltpu.VMEM((2, depth, 2 * head_dim), jnp.bfloat16),
             pltpu.VMEM((owners, 8, row_count), jnp.int32),
             pltpu.VMEM(block, jnp.float32),
             pltpu.VMEM(block, jnp.bfloat16),

time: 65.2 us -> 65.2 us (level)
  no operation moved by 1% of the time
where the time goes in v5:
time: 65.2 us; the launch traced here: 65.1 us
  Pallas kernels  62.1 us (95%)
  local copies, waits for them, and re-layouts  2.94 us (5%)
    pallas_call x1, Pallas kernels, head_body(): pl.pallas_call(functools.partial(head_kernel, owners, depth, head_dim, he...  62.1 us
    unnamed x4, local copies, waits for them, and re-layouts  2.1 us

profile of v5, /device:TPU:0, one launch (start us, length us, event | category | flops | bytes accessed | tf_op | source)
XLA Modules:
  0.0 65.1 jit_solution(13007158472820946533)
XLA Ops:
  0.0 0.0 copy-start
  0.0 0.8 %broadcast_in_dim.4.cl_ref = s32[4,8,256]{2,1,0:T(8,128)S(1)} broadcast(s32[4,256]{1,0:T(4,128)} %bitcast.11), dimensions={0,2} | broadcast | bytes 36864 | tf_op jit(solution)/shard_map/broadcast_in_dim | solution.py:304
  0.8 1.4 %copy.6 = bf16[512,2,512]{2,0,1:T(8,128)(2,1)S(1)} copy(bf16[512,2,512]{2,1,0:T(2,128)(2,1)} %param.4) | data formatting | bytes 2097152 | tf_op args[1]
  2.2 0.0 copy-done
  2.2 62.1 %shard_map.37 = bf16[256,512]{1,0:T(8,128)(2,1)S(1)} custom-call(bf16[256,4096]{1,0:T(8,128)(2,1)S(1)} %bitcast.9, bf16[2,512,512]{2,1,0:T(8,128)(2,1)S(1)} %bitcast.8, s32[4,8,256]{2,1,0:T(8,128)S(1)} %broadcast_in_dim.4.cl_ref), custom_call_target="tpu_custom_call" | custom-call | tf_op jit(solution)/shard_map/pallas_call | solution.py:308
  64.4 0.7 %copy.8 = bf16[1,256,512]{2,1,0:T(8,128)(2,1)} copy(bf16[1,256,512]{2,1,0:T(8,128)(2,1)S(1)} %bitcast.10) | data formatting | bytes 524288
Async XLA Ops:
  0.0 2.2 %copy-start = (bf16[1,256,4096]{2,1,0:T(8,128)(2,1)S(1)}, bf16[1,256,4096]{2,1,0:T(8,128)(2,1)}, u32[]{:S(2)}) copy-start(bf16[1,256,4096]{2,1,0:T(8,128)(2,1)} %param.3) | copy-start | bytes 6291460

commit v6 on v5

--- a/solution.py
+++ b/solution.py
@@ -8,6 +8,7 @@
 from jax.sharding import PartitionSpec as P
 
 CLUSTERS = 64
+LOG2E = 1.4426950408889634
 MESH = pl.DeviceIdType.MESH
 
 
@@ -29,6 +30,8 @@
     side = lax.rem(c, 2)
     near = side != pair
     count = tok_ref.shape[0]
+    short = count // 2
+    cut = depth // 2
     half = tok_ref.shape[1] // 2
     run = half // 2
     quarter = half // 4
@@ -53,8 +56,9 @@
 
     heads = (1 - pair, pair)
 
-    def piece(ctx, at, role):
-        return weights.at[heads[role], pl.ds(pl.multiple_of((ctx * 2 + at) * depth, depth), depth)]
+    def piece(ctx, at, role, e):
+        start = pl.multiple_of((ctx * 2 + at) * depth + e * cut, cut)
+        return weights.at[heads[role], pl.ds(start, cut)]
 
     barrier = pltpu.get_barrier_semaphore()
     others = [at_clu(lax.rem(c + d, owners)) for d in range(1, owners)]
@@ -62,10 +66,12 @@
     for peer in others:
         pl.semaphore_signal(barrier, inc=1, device_id=peer, device_id_type=MESH)
     local = [
-        pltpu.make_async_copy(tok_ref.at[:, held(pair, q)], rows.at[c, q], own_sem.at[q])
-        for q in range(4)
+        pltpu.make_async_copy(
+            tok_ref.at[pl.ds(h * short, short), held(pair, q)], rows.at[c, h, q], own_sem.at[h * 4 + q]
+        )
+        for q in range(4) for h in range(2)
     ]
-    local.append(pltpu.make_async_copy(cl_ref.at[c], ids.at[c], own_sem.at[4]))
+    local.append(pltpu.make_async_copy(cl_ref.at[c], ids.at[c], own_sem.at[8]))
     for copy in local:
         copy.start()
     for role in range(2):
@@ -84,64 +90,67 @@
         mate,
     ]
 
-    def cross():
+    def cross(h):
         turn = jnp.where(near, 0, 1)
         return remote(
-            tok_ref.at[:, held(1 - pair, t)], rows.at[c, t],
-            cross_send.at[0], cross_recv.at[turn], at_clu(2 - pair),
-        )
-
-    def cross_came(n):
-        here = rows.at[blocks[n], t]
-        return remote(here, here, cross_send.at[0], cross_recv.at[n], at_clu(mate))
-
-    def forward(n):
-        here = rows.at[blocks[n], t]
-        return remote(here, here, fwd_send.at[n], fwd_recv.at[n], at_clu(mate))
-
-    def to_mate():
+            tok_ref.at[pl.ds(h * short, short), held(1 - pair, t)], rows.at[c, h, t],
+            cross_send.at[h], cross_recv.at[turn, h], at_clu(2 - pair),
+        )
+
+    def cross_came(n, h):
+        here = rows.at[blocks[n], h, t]
+        return remote(here, here, cross_send.at[h], cross_recv.at[n, h], at_clu(mate))
+
+    def forward(n, h):
+        here = rows.at[blocks[n], h, t]
+        return remote(here, here, fwd_send.at[n, h], fwd_recv.at[n, h], at_clu(mate))
+
+    def to_mate(h):
         return remote(
-            tok_ref.at[:, held(pair, t)], rows.at[c, t],
-            mate_send.at[0], mate_recv.at[0], at_clu(mate),
-        )
-
-    def mate_came():
-        here = rows.at[mate, t]
-        return remote(here, here, mate_send.at[0], mate_recv.at[0], at_clu(mate))
-
-    def shared(n, q, send, recv, peer):
-        here = rows.at[blocks[n], q]
-        return remote(here, here, send.at[n], recv.at[n], peer)
-
-    def to_core(n, q):
-        return shared(n, q, core_send, core_recv, core_peer)
-
-    def to_y(n, q):
-        return shared(n, q, y_send, y_recv, y_peer)
-
-    def to_core_far(n, q):
-        return shared(n, q, far_send, far_recv, core_peer)
-
-    def w_mate(role):
+            tok_ref.at[pl.ds(h * short, short), held(pair, t)], rows.at[c, h, t],
+            mate_send.at[h], mate_recv.at[h], at_clu(mate),
+        )
+
+    def mate_came(h):
+        here = rows.at[mate, h, t]
+        return remote(here, here, mate_send.at[h], mate_recv.at[h], at_clu(mate))
+
+    def shared(n, h, q, send, recv, peer):
+        here = rows.at[blocks[n], h, q]
+        return remote(here, here, send.at[n, h], recv.at[n, h], peer)
+
+    def to_core(n, h, q):
+        return shared(n, h, q, core_send, core_recv, core_peer)
+
+    def to_y(n, h, q):
+        return shared(n, h, q, y_send, y_recv, y_peer)
+
+    def to_core_far(n, h, q):
+        return shared(n, h, q, far_send, far_recv, core_peer)
+
+    def w_mate(role, e):
         return remote(
-            stage.at[role], piece(a, side, role), wm_send.at[role], wm_recv.at[role], at_clu(mate)
-        )
-
-    def w_mate_came(role):
-        here = piece(a, 1 - side, role)
-        return remote(here, here, wm_send.at[role], wm_recv.at[role], at_clu(mate))
-
-    def w_cross(i, ctx, role):
-        here = piece(ctx, side if i == 0 else 1 - side, role)
-        return remote(here, here, wx_send.at[i, role], wx_recv.at[i, role], x_peer)
+            stage.at[role, pl.ds(e * cut, cut)], piece(a, side, role, e),
+            wm_send.at[role, e], wm_recv.at[role, e], at_clu(mate),
+        )
+
+    def w_mate_came(role, e):
+        here = piece(a, 1 - side, role, e)
+        return remote(here, here, wm_send.at[role, e], wm_recv.at[role, e], at_clu(mate))
+
+    def w_cross(i, ctx, role, e):
+        here = piece(ctx, side if i == 0 else 1 - side, role, e)
+        return remote(here, here, wx_send.at[i, role, e], wx_recv.at[i, role, e], x_peer)
 
     def w_pass(role):
-        w_mate_came(role).wait_recv()
-        w_cross(1, a, role).start()
+        for e in range(2):
+            w_mate_came(role, e).wait_recv()
+            w_cross(1, a, role, e).start()
 
     def w_ready(role):
         for i in range(2):
-            w_cross(i, 1 - a, role).wait_recv()
+            for e in range(2):
+                w_cross(i, 1 - a, role, e).wait_recv()
 
     def id_hop(d):
         goal = lax.rem(c + d, owners)
@@ -151,80 +160,91 @@
         source = lax.rem(c + owners - d, owners)
         return remote(ids.at[source], ids.at[source], id_send.at[d - 1], id_recv.at[d - 1], at_clu(source))
 
-    def part_hop(block):
-        return remote(part.at[block], theirs.at[block], part_send.at[block], part_recv.at[block], at_clu(twin))
-
-    cross().start()
-    w_cross(0, a, 0).start()
-    w_mate(0).start()
-    to_mate().start()
-    w_cross(0, a, 1).start()
-    pl.when(jnp.logical_not(near))(lambda: w_mate(1).start())
+    def part_hop(block, h):
+        return remote(
+            part.at[block, h], theirs.at[block, h],
+            part_send.at[block, h], part_recv.at[block, h], at_clu(twin),
+        )
+
+    for h in range(2):
+        cross(h).start()
+    for role in range(2):
+        for e in range(2):
+            w_cross(0, a, role, e).start()
+            w_mate(role, e).start()
+        if role == 0:
+            for h in range(2):
+                to_mate(h).start()
     for d in range(1, owners):
         id_hop(d).start()
 
-    def share(n):
-        to_y(n, t).start()
-        to_core(n, t).start()
+    def share(n, h):
+        to_y(n, h, t).start()
+        to_core(n, h, t).start()
 
     def relay(n):
         q = (1 - y) * 2 + k
-        to_y(n, q).wait_recv()
-        to_core_far(n, q).start()
+        for h in range(2):
+            to_y(n, h, q).wait_recv()
+            to_core_far(n, h, q).start()
 
     def arrive_near(n):
-        cross_came(n).wait_recv()
-        forward(n).start()
-        share(n)
+        for h in range(2):
+            cross_came(n, h).wait_recv()
+            forward(n, h).start()
+            share(n, h)
 
     def arrive_far(n):
-        forward(n).wait_recv()
-        share(n)
-
-    def whole(block):
-        return jnp.concatenate([rows[block, q] for q in range(4)], axis=1)
-
-    def give(block):
-        given = jnp.dot(whole(block), weights[1 - pair], preferred_element_type=jnp.float32)
-        part[block] = given.astype(jnp.bfloat16)
-        part_hop(block).start()
+        for h in range(2):
+            forward(n, h).wait_recv()
+            share(n, h)
+
+    def whole(block, h):
+        return jnp.concatenate([rows[block, h, q] for q in range(4)], axis=1)
+
+    def give(block, h):
+        given = jnp.dot(whole(block, h), weights[1 - pair], preferred_element_type=jnp.float32)
+        part[block, h] = given.astype(jnp.bfloat16)
+        part_hop(block, h).start()
 
     def finish(n):
-        to_core(n, y * 2 + 1 - k).wait_recv()
-        to_core_far(n, (1 - y) * 2 + 1 - k).wait_recv()
-        give(blocks[n])
+        for h in range(2):
+            to_core(n, h, y * 2 + 1 - k).wait_recv()
+            to_core_far(n, h, (1 - y) * 2 + 1 - k).wait_recv()
+            give(blocks[n], h)
 
     pl.when(near)(lambda: arrive_near(0))
     w_pass(0)
-
-    @pl.when(near)
-    def _():
-        arrive_near(1)
-        w_mate(1).start()
-
-    mate_came().wait_recv()
-    share(2)
+    pl.when(near)(lambda: arrive_near(1))
+    for h in range(2):
+        mate_came(h).wait_recv()
+        share(2, h)
     pl.when(jnp.logical_not(near))(lambda: arrive_far(0))
     relay(2)
     for copy in local:
         copy.wait()
     w_ready(0)
-    give(c)
+    for h in range(2):
+        give(c, h)
     finish(2)
     relay(0)
-    pl.when(jnp.logical_not(near))(lambda: arrive_far(1))
     w_pass(1)
     finish(0)
+    pl.when(jnp.logical_not(near))(lambda: arrive_far(1))
     relay(1)
     finish(1)
     w_ready(1)
     for block in range(owners):
-        mine[block] = jnp.dot(whole(block), weights[pair], preferred_element_type=jnp.float32)
+        for h in range(2):
+            mine[block, h] = jnp.dot(whole(block, h), weights[pair], preferred_element_type=jnp.float32)
     for d in range(1, owners):
         id_came(d).wait_recv()
     for block in range(owners):
-        part_hop(block).wait_recv()
-        proj[block] = (mine[block] + theirs[block].astype(jnp.float32)).astype(jnp.bfloat16)
+        for h in range(2):
+            part_hop(block, h).wait_recv()
+            proj[block, h * short : (h + 1) * short] = (
+                mine[block, h] + theirs[block, h].astype(jnp.float32)
+            ).astype(jnp.bfloat16)
 
     def send_reply(goal):
         return remote(
@@ -246,19 +266,19 @@
             scores = lax.dot_general(
                 query, proj[block, :, :head_dim], (((1,), (1,)), ((), ())),
                 preferred_element_type=jnp.float32,
-            ) * score_scale
+            ) * (score_scale * LOG2E)
             admitted = query_ids == ids[block, :1, :]
             if block == goal:
                 at = lax.broadcasted_iota(jnp.int32, (count, count), 0)
                 to = lax.broadcasted_iota(jnp.int32, (count, count), 1)
-                scores = jnp.where(at == to, -100000.0, scores)
+                scores = jnp.where(at == to, -100000.0 * LOG2E, scores)
                 admitted = admitted & (to <= at)
             parts.append(jnp.where(admitted, scores, -1e30))
         top = functools.reduce(jnp.maximum, [jnp.max(p, axis=1, keepdims=True) for p in parts])
         total = jnp.zeros((count, 1), jnp.float32)
         mixed = jnp.zeros((count, head_dim), jnp.float32)
         for block, piece_scores in enumerate(parts):
-            weighed = jnp.exp(piece_scores - top)
+            weighed = jnp.exp2(piece_scores - top)
             total += jnp.sum(weighed, axis=1, keepdims=True)
             mixed += jnp.dot(
                 weighed.astype(jnp.bfloat16), proj[block, :, head_dim:],
@@ -268,22 +288,24 @@
         pl.when(c != goal)(lambda goal=goal: send_reply(goal).start())
         pl.when(c == goal)(lambda goal=goal: keep_reply(goal).start())
 
-    cross().wait_send()
-    to_mate().wait_send()
+    for h in range(2):
+        cross(h).wait_send()
+        to_mate(h).wait_send()
+        for n in range(2):
+            pl.when(near)(lambda n=n, h=h: forward(n, h).wait_send())
+        for n in range(3):
+            to_y(n, h, t).wait_send()
+            to_core(n, h, t).wait_send()
+            to_core_far(n, h, (1 - y) * 2 + k).wait_send()
+        for block in range(owners):
+            part_hop(block, h).wait_send()
     for role in range(2):
-        w_mate(role).wait_send()
-        for i in range(2):
-            w_cross(i, a, role).wait_send()
+        for e in range(2):
+            w_mate(role, e).wait_send()
+            for i in range(2):
+                w_cross(i, a, role, e).wait_send()
     for d in range(1, owners):
         id_hop(d).wait_send()
-    for n in range(2):
-        pl.when(near)(lambda n=n: forward(n).wait_send())
-    for n in range(3):
-        to_y(n, t).wait_send()
-        to_core(n, t).wait_send()
-        to_core_far(n, (1 - y) * 2 + k).wait_send()
-    for block in range(owners):
-        part_hop(block).wait_send()
     for goal in range(owners):
         @pl.when(c != goal)
         def _(goal=goal):
@@ -304,33 +326,33 @@
     labels = jnp.broadcast_to(clusters[0].T[:, None, :], (heads_here, 8, row_count))
     steps = owners - 1
     dma = pltpu.SemaphoreType.DMA
-    block = (owners, row_count, 2 * head_dim)
+    split = (owners, 2, row_count // 2, 2 * head_dim)
     out = pl.pallas_call(
         functools.partial(head_kernel, owners, depth, head_dim, head_dim ** (-0.5)),
         out_shape=jax.ShapeDtypeStruct((row_count, proj_width), jnp.bfloat16),
         in_specs=[pl.BlockSpec(memory_space=space) for space in (pl.ANY, pltpu.VMEM, pl.ANY)],
         out_specs=pl.BlockSpec(memory_space=pl.ANY),
         scratch_shapes=[
-            pltpu.VMEM((owners, 4, row_count, width // 8), jnp.bfloat16),
+            pltpu.VMEM((owners, 2, 4, row_count // 2, width // 8), jnp.bfloat16),
             pltpu.VMEM((2, width // 2, 2 * head_dim), jnp.bfloat16),
             pltpu.VMEM((2, depth, 2 * head_dim), jnp.bfloat16),
             pltpu.VMEM((owners, 8, row_count), jnp.int32),
-            pltpu.VMEM(block, jnp.float32),
-            pltpu.VMEM(block, jnp.bfloat16),
-            pltpu.VMEM(block, jnp.bfloat16),
-            pltpu.VMEM(block, jnp.bfloat16),
+            pltpu.VMEM(split, jnp.float32),
+            pltpu.VMEM(split, jnp.bfloat16),
+            pltpu.VMEM(split, jnp.bfloat16),
+            pltpu.VMEM((owners, row_count, 2 * head_dim), jnp.bfloat16),
             pltpu.VMEM((owners, row_count, head_dim), jnp.bfloat16),
-            dma((5,)),
+            dma((9,)),
+            dma((2, 2)), dma((2, 2)),
+            dma((2, 2, 2)), dma((2, 2, 2)),
+            dma((steps,)), dma((steps,)),
+            dma((2,)), dma((2, 2)),
+            dma((2, 2)), dma((2, 2)),
             dma((2,)), dma((2,)),
-            dma((2, 2)), dma((2, 2)),
-            dma((steps,)), dma((steps,)),
-            dma((1,)), dma((2,)),
-            dma((2,)), dma((2,)),
-            dma((1,)), dma((1,)),
-            dma((3,)), dma((3,)),
-            dma((3,)), dma((3,)),
-            dma((3,)), dma((3,)),
-            dma((owners,)), dma((owners,)),
+            dma((3, 2)), dma((3, 2)),
+            dma((3, 2)), dma((3, 2)),
+            dma((3, 2)), dma((3, 2)),
+            dma((owners, 2)), dma((owners, 2)),
             dma((owners,)), dma((owners,)),
         ],
         compiler_params=pltpu.CompilerParams(

time: 65.2 us -> 68 us (1.043)
  Pallas kernels: 62.1 us -> 64.8 us
    pallas_call x1, Pallas kernels: 62.1 us -> 64.8 us  [head_body(): pl.pallas_call(functools.partial(head_kernel, owners, depth, head_dim, he...]
where the time goes in v6:
time: 68 us; the launch traced here: 67.8 us
  Pallas kernels  64.8 us (95%)
  local copies, waits for them, and re-layouts  2.94 us (4%)
    pallas_call x1, Pallas kernels, head_body(): pl.pallas_call(functools.partial(head_kernel, owners, depth, head_dim, he...  64.8 us
    unnamed x4, local copies, waits for them, and re-layouts  2.1 us

profile of v6, /device:TPU:0, one launch (start us, length us, event | category | flops | bytes accessed | tf_op | source)
XLA Modules:
  0.0 67.8 jit_solution(10976865458594139600)
XLA Ops:
  0.0 0.0 copy-start
  0.0 0.8 %broadcast_in_dim.4.cl_ref = s32[4,8,256]{2,1,0:T(8,128)S(1)} broadcast(s32[4,256]{1,0:T(4,128)} %bitcast.11), dimensions={0,2} | broadcast | bytes 36864 | tf_op jit(solution)/shard_map/broadcast_in_dim | solution.py:326
  0.8 1.4 %copy.6 = bf16[512,2,512]{2,0,1:T(8,128)(2,1)S(1)} copy(bf16[512,2,512]{2,1,0:T(2,128)(2,1)} %param.4) | data formatting | bytes 2097152 | tf_op args[1]
  2.2 0.0 copy-done
  2.2 64.8 %shard_map.37 = bf16[256,512]{1,0:T(8,128)(2,1)S(1)} custom-call(bf16[256,4096]{1,0:T(8,128)(2,1)S(1)} %bitcast.9, bf16[2,512,512]{2,1,0:T(8,128)(2,1)S(1)} %bitcast.8, s32[4,8,256]{2,1,0:T(8,128)S(1)} %broadcast_in_dim.4.cl_ref), custom_call_target="tpu_custom_call" | custom-call | tf_op jit(solution)/shard_map/pallas_call | solution.py:330
  67.1 0.7 %copy.8 = bf16[1,256,512]{2,1,0:T(8,128)(2,1)} copy(bf16[1,256,512]{2,1,0:T(8,128)(2,1)S(1)} %bitcast.10) | data formatting | bytes 524288
Async XLA Ops:
  0.0 2.2 %copy-start = (bf16[1,256,4096]{2,1,0:T(8,128)(2,1)S(1)}, bf16[1,256,4096]{2,1,0:T(8,128)(2,1)}, u32[]{:S(2)}) copy-start(bf16[1,256,4096]{2,1,0:T(8,128)(2,1)} %param.3) | copy-start | bytes 6291460

commit v7 on v6

--- a/solution.py
+++ b/solution.py
@@ -171,7 +171,8 @@
     for role in range(2):
         for e in range(2):
             w_cross(0, a, role, e).start()
-            w_mate(role, e).start()
+            if role == 0:
+                w_mate(role, e).start()
         if role == 0:
             for h in range(2):
                 to_mate(h).start()
@@ -216,6 +217,8 @@
     pl.when(near)(lambda: arrive_near(0))
     w_pass(0)
     pl.when(near)(lambda: arrive_near(1))
+    for e in range(2):
+        w_mate(1, e).start()
     for h in range(2):
         mate_came(h).wait_recv()
         share(2, h)
@@ -235,15 +238,15 @@
     finish(1)
     w_ready(1)
     for block in range(owners):
-        for h in range(2):
-            mine[block, h] = jnp.dot(whole(block, h), weights[pair], preferred_element_type=jnp.float32)
+        both = jnp.concatenate([whole(block, h) for h in range(2)], axis=0)
+        mine[block] = jnp.dot(both, weights[pair], preferred_element_type=jnp.float32)
     for d in range(1, owners):
         id_came(d).wait_recv()
     for block in range(owners):
         for h in range(2):
             part_hop(block, h).wait_recv()
             proj[block, h * short : (h + 1) * short] = (
-                mine[block, h] + theirs[block, h].astype(jnp.float32)
+                mine[block, h * short : (h + 1) * short] + theirs[block, h].astype(jnp.float32)
             ).astype(jnp.bfloat16)
 
     def send_reply(goal):
@@ -337,7 +340,7 @@
             pltpu.VMEM((2, width // 2, 2 * head_dim), jnp.bfloat16),
             pltpu.VMEM((2, depth, 2 * head_dim), jnp.bfloat16),
             pltpu.VMEM((owners, 8, row_count), jnp.int32),
-            pltpu.VMEM(split, jnp.float32),
+            pltpu.VMEM((owners, row_count, 2 * head_dim), jnp.float32),
             pltpu.VMEM(split, jnp.bfloat16),
             pltpu.VMEM(split, jnp.bfloat16),
             pltpu.VMEM((owners, row_count, 2 * head_dim), jnp.bfloat16),

time: 68 us -> 65.2 us (0.959)
  Pallas kernels: 64.8 us -> 62.1 us
    pallas_call x1, Pallas kernels: 64.8 us -> 62.1 us  [head_body(): pl.pallas_call(functools.partial(head_kernel, owners, depth, head_dim, he...]
where the time goes in v7:
time: 65.2 us; the launch traced here: 65 us
  Pallas kernels  62.1 us (95%)
  local copies, waits for them, and re-layouts  2.94 us (5%)
    pallas_call x1, Pallas kernels, head_body(): pl.pallas_call(functools.partial(head_kernel, owners, depth, head_dim, he...  62.1 us
    unnamed x4, local copies, waits for them, and re-layouts  2.1 us

profile of v7, /device:TPU:0, one launch (start us, length us, event | category | flops | bytes accessed | tf_op | source)
XLA Modules:
  0.0 65.0 jit_solution(6869693081526946396)
XLA Ops:
  0.0 0.0 copy-start
  0.0 0.8 %broadcast_in_dim.4.cl_ref = s32[4,8,256]{2,1,0:T(8,128)S(1)} broadcast(s32[4,256]{1,0:T(4,128)} %bitcast.11), dimensions={0,2} | broadcast | bytes 36864 | tf_op jit(solution)/shard_map/broadcast_in_dim | solution.py:329
  0.8 1.4 %copy.6 = bf16[512,2,512]{2,0,1:T(8,128)(2,1)S(1)} copy(bf16[512,2,512]{2,1,0:T(2,128)(2,1)} %param.4) | data formatting | bytes 2097152 | tf_op args[1]
  2.2 0.0 copy-done
  2.2 62.1 %shard_map.37 = bf16[256,512]{1,0:T(8,128)(2,1)S(1)} custom-call(bf16[256,4096]{1,0:T(8,128)(2,1)S(1)} %bitcast.9, bf16[2,512,512]{2,1,0:T(8,128)(2,1)S(1)} %bitcast.8, s32[4,8,256]{2,1,0:T(8,128)S(1)} %broadcast_in_dim.4.cl_ref), custom_call_target="tpu_custom_call" | custom-call | tf_op jit(solution)/shard_map/pallas_call | solution.py:333
  64.3 0.7 %copy.8 = bf16[1,256,512]{2,1,0:T(8,128)(2,1)} copy(bf16[1,256,512]{2,1,0:T(8,128)(2,1)S(1)} %bitcast.10) | data formatting | bytes 524288
Async XLA Ops:
  0.0 2.2 %copy-start = (bf16[1,256,4096]{2,1,0:T(8,128)(2,1)S(1)}, bf16[1,256,4096]{2,1,0:T(8,128)(2,1)}, u32[]{:S(2)}) copy-start(bf16[1,256,4096]{2,1,0:T(8,128)(2,1)} %param.3) | copy-start | bytes 6291460

commit v8 on v7

--- a/solution.py
+++ b/solution.py
@@ -15,7 +15,7 @@
 def head_kernel(
     owners, depth, head_dim, score_scale,
     tok_ref, w_ref, cl_ref, out_ref,
-    rows, weights, stage, ids, mine, part, theirs, proj, reply,
+    rows, weights, stage, marks, ids, mine, part, theirs, proj, reply,
     own_sem, wm_send, wm_recv, wx_send, wx_recv, id_send, id_recv,
     cross_send, cross_recv, fwd_send, fwd_recv, mate_send, mate_recv,
     core_send, core_recv, y_send, y_recv, far_send, far_recv,
@@ -71,9 +71,11 @@
         )
         for q in range(4) for h in range(2)
     ]
-    local.append(pltpu.make_async_copy(cl_ref.at[c], ids.at[c], own_sem.at[8]))
     for copy in local:
         copy.start()
+    for head in range(owners):
+        marks[head] = jnp.broadcast_to(cl_ref[head : head + 1, :], marks.shape[1:])
+    ids[c] = marks[c]
     for role in range(2):
         for kind in range(2):
             lands = pl.ds(kind * head_dim, head_dim)
@@ -154,7 +156,7 @@
 
     def id_hop(d):
         goal = lax.rem(c + d, owners)
-        return remote(cl_ref.at[goal], ids.at[c], id_send.at[d - 1], id_recv.at[d - 1], at_clu(goal))
+        return remote(marks.at[goal], ids.at[c], id_send.at[d - 1], id_recv.at[d - 1], at_clu(goal))
 
     def id_came(d):
         source = lax.rem(c + owners - d, owners)
@@ -231,9 +233,9 @@
         give(c, h)
     finish(2)
     relay(0)
-    w_pass(1)
     finish(0)
     pl.when(jnp.logical_not(near))(lambda: arrive_far(1))
+    w_pass(1)
     relay(1)
     finish(1)
     w_ready(1)
@@ -326,26 +328,26 @@
     depth, _, proj_width = proj_weight.shape
     head_dim = proj_width // heads_here
     kinds = proj_weight.transpose(1, 0, 2)
-    labels = jnp.broadcast_to(clusters[0].T[:, None, :], (heads_here, 8, row_count))
     steps = owners - 1
     dma = pltpu.SemaphoreType.DMA
     split = (owners, 2, row_count // 2, 2 * head_dim)
     out = pl.pallas_call(
         functools.partial(head_kernel, owners, depth, head_dim, head_dim ** (-0.5)),
         out_shape=jax.ShapeDtypeStruct((row_count, proj_width), jnp.bfloat16),
-        in_specs=[pl.BlockSpec(memory_space=space) for space in (pl.ANY, pltpu.VMEM, pl.ANY)],
+        in_specs=[pl.BlockSpec(memory_space=space) for space in (pl.ANY, pltpu.VMEM, pltpu.VMEM)],
         out_specs=pl.BlockSpec(memory_space=pl.ANY),
         scratch_shapes=[
             pltpu.VMEM((owners, 2, 4, row_count // 2, width // 8), jnp.bfloat16),
             pltpu.VMEM((2, width // 2, 2 * head_dim), jnp.bfloat16),
             pltpu.VMEM((2, depth, 2 * head_dim), jnp.bfloat16),
             pltpu.VMEM((owners, 8, row_count), jnp.int32),
+            pltpu.VMEM((owners, 8, row_count), jnp.int32),
             pltpu.VMEM((owners, row_count, 2 * head_dim), jnp.float32),
             pltpu.VMEM(split, jnp.bfloat16),
             pltpu.VMEM(split, jnp.bfloat16),
             pltpu.VMEM((owners, row_count, 2 * head_dim), jnp.bfloat16),
             pltpu.VMEM((owners, row_count, head_dim), jnp.bfloat16),
-            dma((9,)),
+            dma((8,)),
             dma((2, 2)), dma((2, 2)),
             dma((2, 2, 2)), dma((2, 2, 2)),
             dma((steps,)), dma((steps,)),
@@ -361,7 +363,7 @@
         compiler_params=pltpu.CompilerParams(
             collective_id=0, has_side_effects=True, vmem_limit_bytes=40 * 1024 * 1024
         ),
-    )(tokens[0], kinds, labels)
+    )(tokens[0], kinds, clusters[0].T)
     return out[None]
 
 

time: 65.2 us -> 65.3 us (level)
    broadcast_in_dim x1 -> x0, local copies, waits for them, and re-layouts: 0.84 us -> none  [head_body(): jnp.broadcast_to(clusters[0].T[:, None, :], (heads_here, 8, row_count))]
    unnamed x4 -> x6, local copies, waits for them, and re-layouts: 2.1 us -> 2.62 us
where the time goes in v8:
time: 65.3 us; the launch traced here: 65.1 us
  Pallas kernels  62.5 us (96%)
  local copies, waits for them, and re-layouts  2.62 us (4%)
    pallas_call x1, Pallas kernels, head_body(): pl.pallas_call(functools.partial(head_kernel, owners, depth, head_dim, he...  62.5 us
    unnamed x6, local copies, waits for them, and re-layouts  2.62 us

profile of v8, /device:TPU:0, one launch (start us, length us, event | category | flops | bytes accessed | tf_op | source)
XLA Modules:
  0.0 65.1 jit_solution(14423409001686709453)
XLA Ops:
  0.0 0.0 copy-start.1
  0.0 0.0 copy-start
  0.0 1.5 %copy.6 = bf16[512,2,512]{2,0,1:T(8,128)(2,1)S(1)} copy(bf16[512,2,512]{2,1,0:T(2,128)(2,1)} %param.4) | data formatting | bytes 2097152 | tf_op args[1]
  1.5 0.0 copy-done.1
  1.6 0.4 copy-done
  1.9 62.5 %shard_map.37 = bf16[256,512]{1,0:T(8,128)(2,1)S(1)} custom-call(bf16[256,4096]{1,0:T(8,128)(2,1)S(1)} %bitcast.9, bf16[2,512,512]{2,1,0:T(8,128)(2,1)S(1)} %bitcast.8, s32[4,256]{1,0:T(4,128)S(1)} %bitcast.11), custom_call_target="tpu_custom_call" | custom-call | tf_op jit(solution)/shard_map/pallas_call | solution.py:334
  64.4 0.7 %copy.8 = bf16[1,256,512]{2,1,0:T(8,128)(2,1)} copy(bf16[1,256,512]{2,1,0:T(8,128)(2,1)S(1)} %bitcast.10) | data formatting | bytes 524288
Async XLA Ops:
  0.0 1.5 %copy-start.1 = (s32[1,256,4]{1,2,0:T(4,128)S(1)}, s32[1,256,4]{1,2,0:T(4,128)}, u32[]{:S(2)}) copy-start(s32[1,256,4]{1,2,0:T(4,128)} %param.5) | copy-start | bytes 12292
  0.0 1.9 %copy-start = (bf16[1,256,4096]{2,1,0:T(8,128)(2,1)S(1)}, bf16[1,256,4096]{2,1,0:T(8,128)(2,1)}, u32[]{:S(2)}) copy-start(bf16[1,256,4096]{2,1,0:T(8,128)(2,1)} %param.3) | copy-start | bytes 6291460

commit v9 on v8

--- a/solution.py
+++ b/solution.py
@@ -279,17 +279,15 @@
                 scores = jnp.where(at == to, -100000.0 * LOG2E, scores)
                 admitted = admitted & (to <= at)
             parts.append(jnp.where(admitted, scores, -1e30))
-        top = functools.reduce(jnp.maximum, [jnp.max(p, axis=1, keepdims=True) for p in parts])
-        total = jnp.zeros((count, 1), jnp.float32)
-        mixed = jnp.zeros((count, head_dim), jnp.float32)
+        top = jnp.max(functools.reduce(jnp.maximum, parts), axis=1, keepdims=True)
+        mixed = jnp.zeros((count, 2 * head_dim), jnp.float32)
         for block, piece_scores in enumerate(parts):
-            weighed = jnp.exp2(piece_scores - top)
-            total += jnp.sum(weighed, axis=1, keepdims=True)
-            mixed += jnp.dot(
-                weighed.astype(jnp.bfloat16), proj[block, :, head_dim:],
-                preferred_element_type=jnp.float32,
+            weighed = jnp.exp2(piece_scores - top).astype(jnp.bfloat16)
+            summands = jnp.concatenate(
+                [proj[block, :, head_dim:], jnp.ones((count, head_dim), jnp.bfloat16)], axis=1
             )
-        reply[goal] = (mixed / total).astype(jnp.bfloat16)
+            mixed += jnp.dot(weighed, summands, preferred_element_type=jnp.float32)
+        reply[goal] = (mixed[:, :head_dim] / mixed[:, head_dim:]).astype(jnp.bfloat16)
         pl.when(c != goal)(lambda goal=goal: send_reply(goal).start())
         pl.when(c == goal)(lambda goal=goal: keep_reply(goal).start())
 

time: 65.3 us -> 65.4 us (level)
  no operation moved by 1% of the time
where the time goes in v9:
time: 65.4 us; the launch traced here: 65.3 us
  Pallas kernels  62.7 us (96%)
  local copies, waits for them, and re-layouts  2.62 us (4%)
    pallas_call x1, Pallas kernels, head_body(): pl.pallas_call(functools.partial(head_kernel, owners, depth, head_dim, he...  62.7 us
    unnamed x6, local copies, waits for them, and re-layouts  2.62 us

profile of v9, /device:TPU:0, one launch (start us, length us, event | category | flops | bytes accessed | tf_op | source)
XLA Modules:
  0.0 65.3 jit_solution(14395901435790475279)
XLA Ops:
  0.0 0.0 copy-start.1
  0.0 0.0 copy-start
  0.0 1.5 %copy.6 = bf16[512,2,512]{2,0,1:T(8,128)(2,1)S(1)} copy(bf16[512,2,512]{2,1,0:T(2,128)(2,1)} %param.4) | data formatting | bytes 2097152 | tf_op args[1]
  1.5 0.0 copy-done.1
  1.6 0.4 copy-done
  1.9 62.7 %shard_map.37 = bf16[256,512]{1,0:T(8,128)(2,1)S(1)} custom-call(bf16[256,4096]{1,0:T(8,128)(2,1)S(1)} %bitcast.9, bf16[2,512,512]{2,1,0:T(8,128)(2,1)S(1)} %bitcast.8, s32[4,256]{1,0:T(4,128)S(1)} %bitcast.11), custom_call_target="tpu_custom_call" | custom-call | tf_op jit(solution)/shard_map/pallas_call | solution.py:332
  64.6 0.7 %copy.8 = bf16[1,256,512]{2,1,0:T(8,128)(2,1)} copy(bf16[1,256,512]{2,1,0:T(8,128)(2,1)S(1)} %bitcast.10) | data formatting | bytes 524288
Async XLA Ops:
  0.0 1.5 %copy-start.1 = (s32[1,256,4]{1,2,0:T(4,128)S(1)}, s32[1,256,4]{1,2,0:T(4,128)}, u32[]{:S(2)}) copy-start(s32[1,256,4]{1,2,0:T(4,128)} %param.5) | copy-start | bytes 12292
  0.0 1.9 %copy-start = (bf16[1,256,4096]{2,1,0:T(8,128)(2,1)S(1)}, bf16[1,256,4096]{2,1,0:T(8,128)(2,1)}, u32[]{:S(2)}) copy-start(bf16[1,256,4096]{2,1,0:T(8,128)(2,1)} %param.3) | copy-start | bytes 6291460

commit v10 on v9

--- a/solution.py
+++ b/solution.py
@@ -217,10 +217,10 @@
             give(blocks[n], h)
 
     pl.when(near)(lambda: arrive_near(0))
+    w_mate(1, 0).start()
     w_pass(0)
     pl.when(near)(lambda: arrive_near(1))
-    for e in range(2):
-        w_mate(1, e).start()
+    w_mate(1, 1).start()
     for h in range(2):
         mate_came(h).wait_recv()
         share(2, h)

time: 65.4 us -> 65.4 us (level)
  no operation moved by 1% of the time
where the time goes in v10:
time: 65.4 us; the launch traced here: 65.3 us
  Pallas kernels  62.7 us (96%)
  local copies, waits for them, and re-layouts  2.62 us (4%)
    pallas_call x1, Pallas kernels, head_body(): pl.pallas_call(functools.partial(head_kernel, owners, depth, head_dim, he...  62.7 us
    unnamed x6, local copies, waits for them, and re-layouts  2.62 us

profile of v10, /device:TPU:0, one launch (start us, length us, event | category | flops | bytes accessed | tf_op | source)
XLA Modules:
  0.0 65.3 jit_solution(6096641190240268144)
XLA Ops:
  0.0 0.0 copy-start.1
  0.0 0.0 copy-start
  0.0 1.5 %copy.6 = bf16[512,2,512]{2,0,1:T(8,128)(2,1)S(1)} copy(bf16[512,2,512]{2,1,0:T(2,128)(2,1)} %param.4) | data formatting | bytes 2097152 | tf_op args[1]
  1.5 0.0 copy-done.1
  1.6 0.4 copy-done
  1.9 62.7 %shard_map.37 = bf16[256,512]{1,0:T(8,128)(2,1)S(1)} custom-call(bf16[256,4096]{1,0:T(8,128)(2,1)S(1)} %bitcast.9, bf16[2,512,512]{2,1,0:T(8,128)(2,1)S(1)} %bitcast.8, s32[4,256]{1,0:T(4,128)S(1)} %bitcast.11), custom_call_target="tpu_custom_call" | custom-call | tf_op jit(solution)/shard_map/pallas_call | solution.py:332
  64.6 0.7 %copy.8 = bf16[1,256,512]{2,1,0:T(8,128)(2,1)} copy(bf16[1,256,512]{2,1,0:T(8,128)(2,1)S(1)} %bitcast.10) | data formatting | bytes 524288
Async XLA Ops:
  0.0 1.5 %copy-start.1 = (s32[1,256,4]{1,2,0:T(4,128)S(1)}, s32[1,256,4]{1,2,0:T(4,128)}, u32[]{:S(2)}) copy-start(s32[1,256,4]{1,2,0:T(4,128)} %param.5) | copy-start | bytes 12292
  0.0 1.9 %copy-start = (bf16[1,256,4096]{2,1,0:T(8,128)(2,1)S(1)}, bf16[1,256,4096]{2,1,0:T(8,128)(2,1)}, u32[]{:S(2)}) copy-start(bf16[1,256,4096]{2,1,0:T(8,128)(2,1)} %param.3) | copy-start | bytes 6291460
